TPU v7x, 512 devices: a whole 4x4x16 slice. The times are simulated.
512 devices in a mesh: span: 32 (over z, core), mesh: 16 (over y, x).
Axes of the slice: x: 4, y: 4, z: 16, core: 2. Of those that a mesh axis runs over, the one named last changes fastest.
Arguments:
- field: float32 [512, 64, 4096], P('span', None, 'mesh'), may hold values from -6 to 6
- coupling: float32 [512, 64, 4096], P('span', None, 'mesh'), may hold values from -0.5 to 0.5
- advect: float32 [2, 64, 4096], P(None, None, 'mesh'), may hold values from -0.04 to 0.04
- send_rows: int32 [16, 16, 31], P('mesh'), may hold values from 0 to 1023, as said below
- neighbours: int32 [4, 4096], P(None, 'mesh'), may hold values from 0 to 1520, as said below
Outputs:
- evolved: float32 [512, 64, 4096], P('span', None, 'mesh')
Inputs may be any that keep to these rules, and one draw needn't show every extreme that they name: send_rows[p, q, :] lists first, one per edge shared by devices p and q along mesh, the rows 4 e + f (element e of device p, edge f) whose traces q needs, in the order that q's neighbours refer to; the other entries are 0. Two devices share edges only if their mesh indices differ by one modulo 16; each pair shares at most 31 edges and some pair exactly 31. neighbours[f, e] is a row 4 e' + f' of the element's own device, or 1024 + q * 31 + r for slot r of what device q sends, or 1520 for a wall; edge f meets edge (f + 2) mod 4 of its neighbour; every device has wall edges.
All inputs are finite; a program needn't handle non-finite values.
Results may differ from a plain program's by a relative error of at most 0.0003.
Values sent between devices are 32-bit elements; how exact they have to be, the bound alone decides.
No kernel may reach another device: no remote copies, remote signals or barrier semaphores. Data moves between devices by JAX's collectives and lax.ppermute only.
A program may use at most 64 MiB of HBM per device.

v0:
```python
import math

import jax
import jax.numpy as jnp
import numpy as np
from jax import lax
from jax.sharding import PartitionSpec as P

SECTIONS = 2


penalty = 0.3
spread_rate = 0.5


def shifted(block, axis, distance):
    devices = range(lax.axis_size(axis))
    route = [((i - distance) % len(devices), i) for i in devices]
    return lax.ppermute(block, axis, route)


def transform_table(length):
    rows = jnp.arange(length, dtype=jnp.int32)[:, None]
    cols = jnp.arange(length, dtype=jnp.int32)[None, :]
    half = length // 2
    wave = jnp.where(rows <= half, rows, rows - half)
    phase = (wave * cols % length).astype(jnp.float32) * (2.0 * math.pi / length)
    scaled = jnp.where(
        (rows == 0) | (rows == half), 1.0 / math.sqrt(length), math.sqrt(2.0 / length)
    ).astype(jnp.float32)
    return jnp.where(rows <= half, jnp.cos(phase), jnp.sin(phase)) * scaled


def span_factor(first, count, length):
    modes = first + jnp.arange(count, dtype=jnp.int32)
    half = length // 2
    whole_wave = jnp.where(modes <= half, modes, modes - half).astype(jnp.int32)
    wave = whole_wave.astype(jnp.float32)
    smooth = 1.0 - spread_rate * (2.0 * wave / length) ** 2
    return jnp.where(3 * whole_wave <= length, smooth, jnp.zeros_like(smooth))


def derivative_tables():
    index = np.arange(8)
    points = np.cos(np.pi * index / 7.0)
    weights = np.where((index == 0) | (index == 7), 2.0, 1.0) * (-1.0) ** index
    distance = points[:, None] - points[None, :] + np.eye(8)
    matrix = np.outer(weights, 1.0 / weights) / distance * (1.0 - np.eye(8))
    matrix = matrix - np.eye(8) * np.sum(matrix, axis=1)[:, None]
    along_a = np.kron(np.eye(8), matrix)
    along_b = np.kron(matrix, np.eye(8))
    return (jnp.asarray(along_a, dtype=jnp.float32), jnp.asarray(along_b, dtype=jnp.float32))


def apply_table(table, block):
    flat = block.reshape(table.shape[1], -1)
    return jnp.dot(table, flat, precision=lax.Precision.HIGHEST).reshape(block.shape)


def derive(table, block):
    return jnp.einsum("pn,mne->mpe", table, block, precision=lax.Precision.HIGHEST)


def edge_values(block):
    modes, nodes, count = block.shape
    four = block.reshape(modes, 8, 8, count)
    return jnp.stack([four[:, 0], four[:, :, 7], four[:, 7], four[:, :, 0]], axis=1)


def lift_jumps(jump):
    modes = jump.shape[0]
    count = jump.shape[3]
    lifted = jnp.zeros((modes, 8, 8, count), jump.dtype)
    lifted = lifted.at[:, 0, :, :].add(jump[:, 0])
    lifted = lifted.at[:, :, 7, :].add(jump[:, 1])
    lifted = lifted.at[:, 7, :, :].add(jump[:, 2])
    lifted = lifted.at[:, :, 0, :].add(jump[:, 3])
    return lifted.reshape(modes, 64, count)


def operate(spectral, advect, send_rows, neighbours, along_a, along_b):
    modes, nodes, elems = spectral.shape
    length = modes * lax.axis_size("span")
    factor = span_factor(lax.axis_index("span") * modes, modes, length)
    own = edge_values(spectral)
    row_width = 8 * modes
    rows = own.transpose(3, 1, 2, 0).reshape(4 * elems, row_width)
    mesh_count = lax.axis_size("mesh")
    capacity = send_rows.shape[2]
    links = neighbours.T.reshape(-1)
    blank = jnp.zeros((1, row_width), rows.dtype)
    here = lax.axis_index("mesh")
    before_peer = (here - 1) % mesh_count
    after_peer = (here + 1) % mesh_count
    to_after = rows[lax.dynamic_index_in_dim(send_rows[0], after_peer, 0, keepdims=False)]
    to_before = rows[lax.dynamic_index_in_dim(send_rows[0], before_peer, 0, keepdims=False)]
    from_before = shifted(to_after, "mesh", 1)
    from_after = shifted(to_before, "mesh", -1)
    table = jnp.concatenate([rows, from_before, from_after, blank], axis=0)
    offset = links - 4 * elems
    peer = offset // capacity
    within = offset % capacity
    index = jnp.where(
        links < 4 * elems,
        links,
        jnp.where(
            peer == before_peer,
            4 * elems + within,
            jnp.where(peer == after_peer, 4 * elems + capacity + within, 4 * elems + 2 * capacity),
        ),
    )
    outer = table[index].reshape(elems, 4, 8, modes).transpose(3, 1, 2, 0)
    jump = outer - own
    return (
        factor[:, None, None] * spectral
        + advect[0] * derive(along_a, spectral)
        + advect[1] * derive(along_b, spectral)
        + penalty * lift_jumps(jump)
    )


def shards(field, coupling, advect, send_rows, neighbours):
    planes = field.shape[0]
    length = planes * lax.axis_size("span")
    table = transform_table(length)
    inverse = table.T
    along_a, along_b = derivative_tables()
    value = field
    for section in range(SECTIONS):
        mixed = value * (1.0 + coupling)
        spectral = lax.all_to_all(
            apply_table(
                table, lax.all_to_all(mixed, "span", split_axis=1, concat_axis=0, tiled=True)
            ),
            "span",
            split_axis=0,
            concat_axis=1,
            tiled=True,
        )
        updated = operate(spectral, advect, send_rows, neighbours, along_a, along_b)
        value = lax.all_to_all(
            apply_table(
                inverse, lax.all_to_all(updated, "span", split_axis=1, concat_axis=0, tiled=True)
            ),
            "span",
            split_axis=0,
            concat_axis=1,
            tiled=True,
        )
    return value


def solution(mesh):
    placed = (
        P("span", None, "mesh"),
        P("span", None, "mesh"),
        P(None, None, "mesh"),
        P("mesh", None, None),
        P(None, "mesh"),
    )
    return jax.shard_map(
        shards, mesh=mesh, in_specs=placed, out_specs=P("span", None, "mesh"), check_vma=False
    )
```

profile of v0, /device:TPU:1, one launch (start us, length us, event | category | flops | bytes accessed | tf_op | source)
XLA Modules:
  0.0 610.8 jit_solution(13766273187088627033)
XLA Ops:
  0.0 3.7 copy_multiply_fusion
  3.7 16.7 %all-to-all-start = ((f32[16,64,256]{2,0,1:T(8,128)}), f32[16,64,256]{2,0,1:T(8,128)S(1)}, u32[]{:S(2)}, u32[]{:S(2)}) async-start(f32[16,64,256]{2,0,1:T(8,128)} %copy_multiply_fusion), calls=%async_computation | async-start | bytes 2097152 | tf_op jit(solution)/shard_map/all_to_all | solution.py:133
  20.6 55.7 %all-to-all-done = f32[16,64,256]{2,0,1:T(8,128)S(1)} async-done(((f32[16,64,256]{2,0,1:T(8,128)}), f32[16,64,256]{2,0,1:T(8,128)S(1)}, u32[]{:S(2)}, u32[]{:S(2)}) %all-to-all-start) | async-done | bytes 1048608 | tf_op jit(solution)/shard_map/all_to_all | solution.py:133
  77.5 7.5 %fusion.13 = f32[512,2,256]{2,0,1:T(8,128)S(1)} fusion(f32[2,256,512]{2,1,0:T(8,128)S(1)} %bitcast.208, f32[512]{0:T(512)S(1)} %fusion.42, s32[512]{0:T(512)S(1)} %add_select_fusion.1, pred[512]{0:T(512)(128)(4,1)S(1)} %iota_compare_fusion.2), kind=kOutput, calls=%fused_computation.27 | convolution fusion | flops 1614807040 | bytes 2101760 | tf_op jit(solution)/shard_map/dot_general | solution.py:57
  85.1 1.8 copy.130
  86.8 4.3 all-to-all-start.1
  92.9 54.0 %all-to-all-done.1 = f32[512,2,256]{2,1,0:T(2,128)S(1)} async-done(((f32[512,2,256]{2,1,0:T(2,128)}), f32[512,2,256]{2,1,0:T(2,128)S(1)}, u32[]{:S(2)}, u32[]{:S(2)}) %all-to-all-start.1) | async-done | bytes 1048608 | tf_op jit(solution)/shard_map/all_to_all | solution.py:131
  148.1 4.4 copy.135
  152.5 3.3 reshape.522
  156.3 6.8 %collective-permute-start.1 = (f32[31,128]{1,0:T(8,128)S(1)}, f32[31,128]{1,0:T(8,128)S(1)}, u32[]{:S(2)}, u32[]{:S(2)}) collective-permute-start(f32[31,128]{1,0:T(8,128)S(1)} %gather_fusion.1), channel_id=1, source_target_pairs={{1,0},{2,1},{3,2},{4,3},{5,4},{6,5},{7,6},{8,7},{9,8},{10,9},{11,1... | collective-permute-start | bytes 47624 | tf_op jit(solution)/shard_map/ppermute | solution.py:19
  163.7 1.9 collective-permute-start
  167.5 4.0 collective-permute-done
  173.0 2.8 gather_fusion.2
  175.9 2.6 reshape.524
  178.4 3.6 copy.137
  185.1 61.4 %all_to_all.132 = f32[16,64,256]{2,0,1:T(8,128)S(1)} all-to-all(f32[16,64,256]{2,0,1:T(8,128)S(1)} %copy.141), channel_id=1, replica_groups=mesh['span'=32,'mesh'=16] {'span'}, dimensions={1} | all-to-all | bytes 2097152 | tf_op jit(solution)/shard_map/all_to_all | solution.py:143
  247.7 6.1 fusion.19
  254.6 59.5 %all_to_all.133 = f32[512,2,256]{2,1,0:T(2,128)S(1)} all-to-all(f32[512,2,256]{2,1,0:T(2,128)S(1)} %copy.144), channel_id=1, replica_groups=mesh['span'=32,'mesh'=16] {'span'}, dimensions={0} | all-to-all | bytes 2097152 | tf_op jit(solution)/shard_map/all_to_all | solution.py:141
  315.0 59.7 %all_to_all.134 = f32[16,64,256]{2,0,1:T(8,128)S(1)} all-to-all(f32[16,64,256]{2,0,1:T(8,128)S(1)} %bitcast_multiply_fusion), channel_id=1, replica_groups=mesh['span'=32,'mesh'=16] {'span'}, dimensions={1} | all-to-all | bytes 2097152 | tf_op jit(solution)/shard_map/all_to_all | solution.py:133
  375.9 7.5 %fusion.15 = f32[512,2,256]{2,0,1:T(8,128)S(1)} fusion(f32[2,256,512]{2,1,0:T(8,128)S(1)} %bitcast.210, f32[512]{0:T(512)S(1)} %copy-done.20, s32[512]{0:T(512)S(1)} %copy-done.17, pred[512]{0:T(512)(128)(4,1)S(1)} %copy-done.23), kind=kOutput, calls=%fused_computation.29 | convolution fusion | flops 1614807040 | bytes 2101760 | tf_op jit(solution)/shard_map/dot_general | solution.py:57
  384.3 59.7 %all_to_all.135 = f32[512,2,256]{2,1,0:T(2,128)S(1)} all-to-all(f32[512,2,256]{2,1,0:T(2,128)S(1)} %copy.149), channel_id=1, replica_groups=mesh['span'=32,'mesh'=16] {'span'}, dimensions={0} | all-to-all | bytes 2097152 | tf_op jit(solution)/shard_map/all_to_all | solution.py:131
  445.0 4.4 copy.155
  449.3 3.2 reshape.530
  455.7 1.9 collective-permute-start.3
  457.7 3.4 collective-permute-start.2
  461.8 2.0 fusion.3
  467.4 2.8 gather_fusion.5
  470.2 2.6 reshape.531
  472.8 3.6 copy.156
  479.3 61.1 %all_to_all.136 = f32[16,64,256]{2,0,1:T(8,128)S(1)} all-to-all(f32[16,64,256]{2,0,1:T(8,128)S(1)} %copy.160), channel_id=1, replica_groups=mesh['span'=32,'mesh'=16] {'span'}, dimensions={1} | all-to-all | bytes 2097152 | tf_op jit(solution)/shard_map/all_to_all | solution.py:143
  541.7 6.1 fusion.17
  548.6 59.5 %all_to_all.137 = f32[512,2,256]{2,1,0:T(2,128)S(1)} all-to-all(f32[512,2,256]{2,1,0:T(2,128)S(1)} %copy.163), channel_id=1, replica_groups=mesh['span'=32,'mesh'=16] {'span'}, dimensions={0} | all-to-all | bytes 2097152 | tf_op jit(solution)/shard_map/all_to_all | solution.py:141
  (125 shorter events, 31.9 us)
Async XLA Ops:
  3.7 72.5 %all-to-all-start = ((f32[16,64,256]{2,0,1:T(8,128)}), f32[16,64,256]{2,0,1:T(8,128)S(1)}, u32[]{:S(2)}, u32[]{:S(2)}) async-start(f32[16,64,256]{2,0,1:T(8,128)} %copy_multiply_fusion), calls=%async_computation | async-start | bytes 2097152 | tf_op jit(solution)/shard_map/all_to_all | solution.py:133
  20.5 64.5 %copy-start.22 = (pred[512]{0:T(512)(128)(4,1)}, pred[512]{0:T(512)(128)(4,1)S(1)}, u32[]{:S(2)}) copy-start(pred[512]{0:T(512)(128)(4,1)S(1)} %iota_compare_fusion.2) | copy-start | bytes 1540
  20.5 64.5 %copy-start.16 = (s32[512]{0:T(512)}, s32[512]{0:T(512)S(1)}, u32[]{:S(2)}) copy-start(s32[512]{0:T(512)S(1)} %add_select_fusion.1) | copy-start | bytes 6148
  20.5 64.5 %copy-start.19 = (f32[512]{0:T(512)}, f32[512]{0:T(512)S(1)}, u32[]{:S(2)}) copy-start(f32[512]{0:T(512)S(1)} %fusion.42) | copy-start | bytes 6148
  77.5 13.7 %copy-start.14 = (s32[4,256]{1,0:T(4,128)S(1)}, s32[4,256]{1,0:T(4,128)}, u32[]{:S(2)}) copy-start(s32[4,256]{1,0:T(4,128)} %param.27) | copy-start | bytes 12292
  77.5 14.8 %copy-start.12 = (f32[2,64,256]{2,1,0:T(8,128)S(1)}, f32[2,64,256]{2,1,0:T(8,128)}, u32[]{:S(2)}) copy-start(f32[2,64,256]{2,1,0:T(8,128)} %param.25) | copy-start | bytes 393220
  86.8 60.1 %all-to-all-start.1 = ((f32[512,2,256]{2,1,0:T(2,128)}), f32[512,2,256]{2,1,0:T(2,128)S(1)}, u32[]{:S(2)}, u32[]{:S(2)}) async-start(f32[512,2,256]{2,1,0:T(2,128)} %copy.130), calls=%async_computation.1 | async-start | bytes 2097152 | tf_op jit(solution)/shard_map/all_to_all | solution.py:131
  147.2 0.9 copy-start.5
  147.2 0.9 copy-start.7
  152.5 13.9 %copy-start.9 = (f32[64,256]{1,0:T(8,128)S(1)}, f32[64,256]{1,0:T(8,128)}, u32[]{:S(2)}) copy-start(f32[64,256]{1,0:T(8,128)} %get-tuple-element.110) | copy-start | bytes 196612
  152.5 13.9 %copy-start.11 = (f32[64,64,1]{1,0,2:T(8,128)S(1)}, f32[64,64,1]{1,0,2:T(8,128)}, u32[]{:S(2)}) copy-start(f32[64,64,1]{1,0,2:T(8,128)} %constant.323) | copy-start | bytes 49156
  156.3 11.2 %collective-permute-start.1 = (f32[31,128]{1,0:T(8,128)S(1)}, f32[31,128]{1,0:T(8,128)S(1)}, u32[]{:S(2)}, u32[]{:S(2)}) collective-permute-start(f32[31,128]{1,0:T(8,128)S(1)} %gather_fusion.1), channel_id=1, source_target_pairs={{1,0},{2,1},{3,2},{4,3},{5,4},{6,5},{7,6},{8,7},{9,8},{10,9},{11,1... | collective-permute-start | bytes 47624 | tf_op jit(solution)/shard_map/ppermute | solution.py:19
  163.7 7.8 %collective-permute-start = (f32[31,128]{1,0:T(8,128)S(1)}, f32[31,128]{1,0:T(8,128)S(1)}, u32[]{:S(2)}, u32[]{:S(2)}) collective-permute-start(f32[31,128]{1,0:T(8,128)S(1)} %gather_fusion), channel_id=1, source_target_pairs={{15,0},{0,1},{1,2},{2,3},{3,4},{4,5},{5,6},{6,7},{7,8},{8,9},{9,10... | collective-permute-start | bytes 47624 | tf_op jit(solution)/shard_map/ppermute | solution.py:19
  178.4 3.6 copy-start.6
  178.4 3.6 copy-start.8
  182.0 0.8 copy-start.10
  185.1 62.6 %copy-start.17 = (s32[512]{0:T(512)S(1)}, s32[512]{0:T(512)}, u32[]{:S(2)}) copy-start(s32[512]{0:T(512)} %copy-done.16) | copy-start | bytes 6148
  185.1 62.6 %copy-start.20 = (f32[512]{0:T(512)S(1)}, f32[512]{0:T(512)}, u32[]{:S(2)}) copy-start(f32[512]{0:T(512)} %copy-done.19) | copy-start | bytes 6148
  185.1 62.6 %copy-start.23 = (pred[512]{0:T(512)(128)(4,1)S(1)}, pred[512]{0:T(512)(128)(4,1)}, u32[]{:S(2)}) copy-start(pred[512]{0:T(512)(128)(4,1)} %copy-done.22) | copy-start | bytes 1540
  253.8 60.5 %copy-start = (f32[16,64,256]{2,1,0:T(8,128)S(1)}, f32[16,64,256]{2,1,0:T(8,128)}, u32[]{:S(2)}) copy-start(f32[16,64,256]{2,1,0:T(8,128)} %param.24) | copy-start | bytes 3145732
  444.2 0.6 copy-start.1
  444.2 0.7 copy-start.3
  453.8 12.0 %copy-start.15 = (f32[1,128]{1,0:T(1,128)S(1)}, f32[1,128]{1,0:T(1,128)}, u32[]{:S(2)}) copy-start(f32[1,128]{1,0:T(1,128)} %broadcast.433) | copy-start | bytes 1540
  455.7 8.0 %collective-permute-start.3 = (f32[31,128]{1,0:T(8,128)}, f32[31,128]{1,0:T(8,128)S(1)}, u32[]{:S(2)}, u32[]{:S(2)}) collective-permute-start(f32[31,128]{1,0:T(8,128)} %gather_fusion.4), channel_id=1, source_target_pairs={{1,0},{2,1},{3,2},{4,3},{5,4},{6,5},{7,6},{8,7},{9,8},{10,9},{11,1... | collective-permute-start | bytes 47624 | tf_op jit(solution)/shard_map/ppermute | solution.py:19
  457.7 8.1 %collective-permute-start.2 = (f32[31,128]{1,0:T(8,128)}, f32[31,128]{1,0:T(8,128)}, u32[]{:S(2)}, u32[]{:S(2)}) collective-permute-start(f32[31,128]{1,0:T(8,128)} %gather_fusion.3), channel_id=1, source_target_pairs={{15,0},{0,1},{1,2},{2,3},{3,4},{4,5},{5,6},{6,7},{7,8},{8,9},{9,10... | collective-permute-start | bytes 47624 | tf_op jit(solution)/shard_map/ppermute | solution.py:19
  463.8 0.6 copy-start.13
  472.8 3.6 copy-start.2
  472.8 3.6 copy-start.4
  479.3 62.4 %copy-start.18 = (s32[512]{0:T(512)S(1)}, s32[512]{0:T(512)}, u32[]{:S(2)}) copy-start(s32[512]{0:T(512)} %copy-done.16) | copy-start | bytes 6148
  479.3 62.4 %copy-start.21 = (f32[512]{0:T(512)S(1)}, f32[512]{0:T(512)}, u32[]{:S(2)}) copy-start(f32[512]{0:T(512)} %copy-done.19) | copy-start | bytes 6148
  479.3 62.4 %copy-start.24 = (pred[512]{0:T(512)(128)(4,1)S(1)}, pred[512]{0:T(512)(128)(4,1)}, u32[]{:S(2)}) copy-start(pred[512]{0:T(512)(128)(4,1)} %copy-done.22) | copy-start | bytes 1540
where the time goes:
time: 620 us; the launch traced here: 611 us
  blocking collectives  361 us (58%)
  waiting for transfers between devices  115 us (19%)
  local copies, waits for them, and re-layouts  58.8 us (9%)
  starting transfers between devices  35.1 us (6%)
  matrix products  33.6 us (5%)
    all_to_all x2, blocking collectives, shards(): lax.all_to_all(updated, 'span', split_axis=1, concat_axis=0, tiled=True)  122 us
    all_to_all x2, blocking collectives, shards(): lax.all_to_all(apply_table(inverse, lax.all_to_all(updated, 'span', split...  119 us
    all_to_all x1, blocking collectives, shards(): lax.all_to_all(apply_table(table, lax.all_to_all(mixed, 'span', split_axi...  59.7 us
    all_to_all x1, blocking collectives, shards(): lax.all_to_all(mixed, 'span', split_axis=1, concat_axis=0, tiled=True)  59.7 us
    all_to_all x1, waiting for transfers between devices, shards(): lax.all_to_all(mixed, 'span', split_axis=1, concat_axis=0, tiled=True)  55.7 us
    all_to_all x1, waiting for transfers between devices, shards(): lax.all_to_all(apply_table(table, lax.all_to_all(mixed, 'span', split_axi...  54 us
    dot_general x4, matrix products, apply_table(): jnp.dot(table, flat, precision=lax.Precision.HIGHEST).reshape(block.shape)  27.2 us
    all_to_all x1, starting transfers between devices, shards(): lax.all_to_all(mixed, 'span', split_axis=1, concat_axis=0, tiled=True)  16.7 us
  transfers between devices with their start and end apart: 6, of which 4 were waited for; matrix products, arithmetic and copies ran while one was open for 1% of the time, Pallas kernels for 0%

commit v1 on v0

v1 whole, which is shorter than its diff:
```python
import functools

import jax
import jax.numpy as jnp
import numpy as np
from jax import lax
from jax.experimental import pallas as pl
from jax.experimental.pallas import tpu as pltpu
from jax.sharding import PartitionSpec as P


NZ = 512
PLANES = 16
PEN = 0.3
LOW = 128

EDGE_B = (
    [(t, 0) for t in range(8)]
    + [(t, 7) for t in range(8)]
    + [(1, 1)] + [(0, t) for t in range(1, 7)] + [(6, 1)]
    + [(1, 6)] + [(7, t) for t in range(1, 7)] + [(6, 6)]
)
B_NODES = [8 * b + a for a, b in EDGE_B]
I_NODES = [n for n in range(64) if n not in B_NODES]


def split_table(table):
    high = table.astype(jnp.bfloat16)
    low = (table - np.asarray(high, np.float64)).astype(jnp.bfloat16)
    return np.asarray(high), np.asarray(low)


def filter_table():
    wave = np.arange(NZ // 2 + 1)
    keep = np.where(3 * wave <= NZ, 1.0 - 0.5 * (2.0 * wave / NZ) ** 2, 0.0)
    fold = np.where((wave == 0) | (wave == NZ // 2), 1.0, 2.0) / NZ
    lag = np.arange(NZ)
    phase = 2.0 * np.pi * ((wave[:, None] * lag[None, :]) % NZ) / NZ
    row = np.sum((keep * fold)[:, None] * np.cos(phase), axis=0)
    return row[(lag[:, None] - lag[None, :]) % NZ]


def derivative_tables():
    index = np.arange(8)
    points = np.cos(np.pi * index / 7.0)
    weights = np.where((index == 0) | (index == 7), 2.0, 1.0) * (-1.0) ** index
    distance = points[:, None] - points[None, :] + np.eye(8)
    matrix = np.outer(weights, 1.0 / weights) / distance * (1.0 - np.eye(8))
    matrix = matrix - np.eye(8) * np.sum(matrix, axis=1)[:, None]
    return np.kron(np.eye(8), matrix), np.kron(matrix, np.eye(8))


def edge_count():
    count = np.zeros(64)
    for n in range(64):
        a, b = n % 8, n // 8
        count[n] = (a == 0) + (a == 7) + (b == 0) + (b == 7)
    return count


def lane_node(lane):
    which, rest = divmod(lane, 64)
    half, i = divmod(rest, 32)
    return half, (B_NODES if which == 0 else I_NODES)[i]


def order_table():
    table = np.zeros((128, 128))
    for lane in range(128):
        half, node = lane_node(lane)
        table[lane, 64 * half + node] = 1.0
    return table


def lane_tables():
    along_a, along_b = derivative_tables()
    out = [np.zeros((128, 128)) for _ in range(2)]
    for k, matrix in enumerate((along_a, along_b)):
        for p in range(128):
            for n in range(128):
                hp, np_ = lane_node(p)
                hn, nn = lane_node(n)
                if hp == hn:
                    out[k][n, p] = matrix[np_, nn]
    count = np.array([edge_count()[lane_node(p)[1]] for p in range(128)])
    return out[0], out[1], count


def iota(shape, axis):
    return lax.broadcasted_iota(jnp.int32, shape, axis)


def halves(x):
    high = x.astype(jnp.bfloat16)
    return high, (x - high.astype(jnp.float32)).astype(jnp.bfloat16)


def dot(a, b):
    return jnp.dot(a, b, preferred_element_type=jnp.float32)


def dot3(ah, al, bh, bl):
    return dot(ah, bh) + dot(ah, bl) + dot(al, bh)


def stack_halves(x):
    return jnp.concatenate([x[:, :LOW], x[:, LOW:]], axis=0)


def call(kernel, outs, flops, limit=16):
    def run(*args):
        moved = sum(a.size * a.dtype.itemsize for a in args)
        moved += sum(int(np.prod(o[0])) * 4 for o in outs)
        shapes = [jax.ShapeDtypeStruct(o[0], o[1]) for o in outs]
        result = pl.pallas_call(
            kernel,
            out_shape=shapes if len(shapes) > 1 else shapes[0],
            compiler_params=pltpu.CompilerParams(vmem_limit_bytes=limit * 2**20),
            cost_estimate=pl.CostEstimate(flops=flops, bytes_accessed=moved, transcendentals=0),
        )(*args)
        return result

    return run


def pack_kernel(field_ref, coupling_ref, order_ref, out_ref):
    order = order_ref[...]
    inner = order[64:]
    for j in range(PLANES):
        c = coupling_ref[j]
        x = stack_halves(field_ref[j] * (1.0 + c))
        xh, xl = halves(x)
        out_ref[pl.ds(j, LOW, stride=24), :] = (dot(order, xh) + dot(order, xl)).T
    for j in range(8):
        parts = []
        for up in (0, 8):
            ch, cl = halves(stack_halves(coupling_ref[j + up]))
            parts.append(dot(inner, ch) + dot(inner, cl))
        out_ref[pl.ds(16 + j, LOW, stride=24), :] = jnp.concatenate(parts, axis=0).T


def one_hot_rows(index_ref, width):
    index = index_ref[...]
    hot = iota((index.shape[0], width), 1) == index
    return jnp.where(hot, 1.0, 0.0).astype(jnp.bfloat16)


def one_hot_cols(index_ref, first, count):
    index = index_ref[...]
    hot = (iota((count, index.shape[1]), 0) + first) == index
    return jnp.where(hot, 1.0, 0.0).astype(jnp.bfloat16)


NT = (((1,), (1,)), ((), ()))


def dot_nt(a, b):
    return lax.dot_general(a, b, NT, preferred_element_type=jnp.float32)


def sent(trace, pick_ref, sent_ref):
    th, tl = halves(trace)
    pick = one_hot_rows(pick_ref, 1024)
    sent_ref[...] = dot_nt(pick, th) + dot_nt(pick, tl)


def first_traces_kernel(field_ref, coupling_ref, pick_ref, trace_ref, sent_ref, mixed):
    for j in range(PLANES):
        x = field_ref[j] * (1.0 + coupling_ref[j])
        mixed[0, pl.ds(64 * j, 64), :] = x[:, :LOW]
        mixed[1, pl.ds(64 * j, 64), :] = x[:, LOW:]
        trace_ref[pl.ds(8 * j, 8), pl.ds(0, 256)] = x[:8]
        trace_ref[pl.ds(8 * j, 8), pl.ds(512, 256)] = x[56:]
    for h in range(2):
        trace_ref[:, pl.ds(256 + LOW * h, LOW)] = mixed[h, pl.ds(7, 128, stride=8), :]
        trace_ref[:, pl.ds(768 + LOW * h, LOW)] = mixed[h, pl.ds(0, 128, stride=8), :]
    sent(trace_ref[...], pick_ref, sent_ref)


def outer_traces(trace_ref, came_ref, link_ref):
    th, tl = halves(trace_ref[...])
    ch, cl = halves(came_ref[...].T)
    here = one_hot_cols(link_ref, 0, 1024)
    there = one_hot_cols(link_ref, 1024, 64)
    return dot(th, here) + dot(tl, here) + dot(ch, there) + dot(cl, there)


def lifted(outer):
    f0, f1, f2, f3 = (outer[:, 256 * f : 256 * f + 256].reshape(16, 8, 256) for f in range(4))
    t = iota((16, 8, 256), 1)
    first, last = t == 0, t == 7
    g0 = f0 + jnp.where(first, f3[:, 0:1], 0.0) + jnp.where(last, f1[:, 0:1], 0.0)
    g1 = f2 + jnp.where(first, f3[:, 7:8], 0.0) + jnp.where(last, f1[:, 7:8], 0.0)
    ends = first | last
    return g0, g1, jnp.where(ends, 0.0, f3), jnp.where(ends, 0.0, f1)


def first_local_kernel(
    field_ref, coupling_ref, advect_ref, trace_ref, came_ref, link_ref, near_ref, pick_ref, gain_ref, add_ref, lift
):
    for g, part in enumerate(lifted(outer_traces(trace_ref, came_ref, link_ref))):
        lift[:, pl.ds(8 * g, 8), :] = part * PEN
    near = near_ref[...]
    pick = pick_ref[...]
    ad_a, ad_b = advect_ref[0], advect_ref[1]

    def plane(j):
        c = coupling_ref[j]
        xh, xl = halves(field_ref[j] * (1.0 + c))
        parts = dot(near, jnp.concatenate([xh, xl, xh], axis=0))
        ch, cl = halves(c)
        gain = 1.0 + (dot(pick, ch) + dot(pick, cl))
        local = ad_a * parts[0:32] + ad_b * parts[32:64] + parts[64:96] + lift[j]
        return gain, gain * local

    for j in range(8):
        gains, adds = [], []
        for up in (0, 8):
            gain, add = plane(j + up)
            gains.append(stack_halves(gain))
            adds.append(stack_halves(add))
        gain_ref[pl.ds(j, LOW, stride=8), :] = jnp.concatenate(gains, axis=0).T
        add_ref[pl.ds(j, LOW, stride=8), :] = jnp.concatenate(adds, axis=0).T


def second_traces_kernel(value_ref, pick_ref, trace_ref, sent_ref):
    t = iota((8, 256), 0)
    for j in range(8):
        rows = value_ref[pl.ds(j, LOW, stride=8), :].T
        for up in range(2):
            part = rows[64 * up : 64 * up + 64]
            g = [
                jnp.concatenate([part[8 * k : 8 * k + 8], part[32 + 8 * k : 40 + 8 * k]], axis=1) for k in range(4)
            ]
            f3 = jnp.where(t == 0, g[0][0:1], jnp.where(t == 7, g[1][0:1], g[2]))
            f1 = jnp.where(t == 0, g[0][7:8], jnp.where(t == 7, g[1][7:8], g[3]))
            for f, one in enumerate((g[0], f1, g[1], f3)):
                trace_ref[pl.ds(8 * (j + 8 * up), 8), pl.ds(256 * f, 256)] = one
    sent(trace_ref[...], pick_ref, sent_ref)


def second_local_kernel(trace_ref, came_ref, link_ref, lift_ref):
    for g, part in enumerate(lifted(outer_traces(trace_ref, came_ref, link_ref))):
        lift_ref[:, pl.ds(8 * g, 8), :] = part * PEN


def final_kernel(value_ref, lift_ref, back_ref, out_ref):
    back = back_ref[...]
    for j in range(PLANES):
        rows = value_ref[pl.ds(j, LOW, stride=16), :].T
        edge = rows[:64] + stack_halves(lift_ref[j])
        rows = jnp.concatenate([edge, rows[64:]], axis=0)
        rh, rl = halves(rows)
        full = dot(back, rh) + dot(back, rl)
        out_ref[j] = jnp.concatenate([full[:64], full[64:]], axis=1)


def lanes_swapped(x):
    return pltpu.roll(x, 64, x.ndim - 1)


def first_filter_kernel(value_ref, high_ref, low_ref, edge_ref, inner_ref):
    low_lanes = iota((32, 8, LOW), 2) < 64
    for pair in range(2):
        xs = [value_ref[:, 2 * pair + k, pl.ds(0, 16), :].reshape(NZ, LOW) for k in range(2)]
        xh, xl = halves(jnp.concatenate(xs, axis=1))
        y = dot3(high_ref[...], low_ref[...], xh, xl)
        for k in range(2):
            e = 2 * pair + k
            rows = y[:, LOW * k : LOW * k + LOW].reshape(32, 16, LOW)
            up, down = rows[:, :8], rows[:, 8:]
            edge_ref[:, e] = jnp.where(low_lanes, up, lanes_swapped(down.reshape(256, LOW)).reshape(32, 8, LOW))
            inner_ref[:, e] = jnp.where(low_lanes, lanes_swapped(up.reshape(256, LOW)).reshape(32, 8, LOW), down)


def first_inner_kernel(value_ref, inner_ref, slope_ref, advect_ref, out_ref):
    low_lanes = iota((32, 8, LOW), 2) < 64
    slope = slope_ref[...]
    for e in range(4):
        xh, xl = halves(value_ref[:, e, pl.ds(0, 16), :].reshape(NZ, LOW))
        u = dot(jnp.concatenate([xh, xl, xh], axis=1), slope) * advect_ref[pl.ds(e, 1), :]
        v = (u + lanes_swapped(u)).reshape(32, 16, LOW)
        local = jnp.where(low_lanes, v[:, :8], v[:, 8:])
        out_ref[:, e] = (inner_ref[:, e] + local) * (1.0 + value_ref[:, e, pl.ds(16, 8), :])


def second_filter_kernel(edge_ref, inner_ref, high_ref, low_ref, slope_ref, advect_ref, count_ref, out_ref):
    low_lanes = iota((32, 8, LOW), 2) < 64
    slope = slope_ref[...]
    count = count_ref[...]
    for pair in range(2):
        xs = []
        for k in range(2):
            e = 2 * pair + k
            edge, inner = edge_ref[:, e], inner_ref[:, e]
            up = jnp.where(low_lanes, edge, lanes_swapped(inner.reshape(256, LOW)).reshape(32, 8, LOW))
            down = jnp.where(low_lanes, lanes_swapped(edge.reshape(256, LOW)).reshape(32, 8, LOW), inner)
            xs.append(jnp.concatenate([up, down], axis=1).reshape(NZ, LOW))
        xh, xl = halves(jnp.concatenate(xs, axis=1))
        y = dot3(high_ref[...], low_ref[...], xh, xl)
        for k in range(2):
            e = 2 * pair + k
            lanes = slice(LOW * k, LOW * k + LOW)
            u = dot(jnp.concatenate([xh[:, lanes], xl[:, lanes], xh[:, lanes]], axis=1), slope)
            z = y[:, lanes] + u[:, :LOW] * advect_ref[0, pl.ds(e, 1), :] + u[:, LOW:] * advect_ref[1, pl.ds(e, 1), :]
            z = z - xs[k] * count
            out_ref[:, e] = z.reshape(32, 16, LOW)


def stacked3(table, axis):
    high, low = split_table(table)
    return np.concatenate([high, high, low], axis=axis)


def exchange(x):
    return lax.all_to_all(x, "span", split_axis=0, concat_axis=0, tiled=True)


def shifted(block, distance):
    devices = lax.axis_size("mesh")
    return lax.ppermute(block, "mesh", [((i - distance) % devices, i) for i in range(devices)])


def link_tables(send_rows, neighbours):
    elems = neighbours.shape[1]
    capacity = send_rows.shape[2]
    count = lax.axis_size("mesh")
    here = lax.axis_index("mesh")
    before, after = (here - 1) % count, (here + 1) % count

    def lane(v):
        return (v % 4) * elems + v // 4

    def rows(peer):
        chosen = lax.dynamic_index_in_dim(send_rows[0], peer, 0, keepdims=False)
        return jnp.pad(lane(chosen), (0, 32 - capacity))

    picks = jnp.concatenate([rows(after), rows(before)])[:, None]
    links = neighbours.reshape(1, 4 * elems)
    offset = links - 4 * elems
    peer, within = offset // capacity, offset % capacity
    index = jnp.where(
        links < 4 * elems,
        lane(links),
        jnp.where(peer == before, 4 * elems + within, jnp.where(peer == after, 4 * elems + 32 + within, -1)),
    )
    return picks.astype(jnp.int32), index.astype(jnp.int32)


def travelled(out):
    return jnp.concatenate([shifted(out[:32], 1), shifted(out[32:], -1)], axis=0)


def shards(field, coupling, advect, send_rows, neighbours):
    high, low = split_table(filter_table())
    order = order_table()
    slope_a, slope_b, count = lane_tables()
    along_a, along_b = derivative_tables()
    pick_b = np.eye(64)[B_NODES]
    near = np.concatenate(
        [along_a[B_NODES], along_b[B_NODES], -PEN * edge_count()[B_NODES][:, None] * pick_b], axis=0
    )
    bf = lambda t: jnp.asarray(t, jnp.bfloat16)
    high, low = jnp.asarray(high), jnp.asarray(low)

    packed = call(pack_kernel, [((LOW * 24, LOW), jnp.float32)], 2 * 10**8)(field, coupling, bf(order))
    arrived = exchange(packed).reshape(32, 4, 24, LOW)

    picks, links = link_tables(send_rows, neighbours)
    trace, out = pl.pallas_call(
        first_traces_kernel,
        out_shape=[jax.ShapeDtypeStruct((128, 1024), jnp.float32), jax.ShapeDtypeStruct((64, 128), jnp.float32)],
        scratch_shapes=[pltpu.VMEM((2, 1024, LOW), jnp.float32)],
        compiler_params=pltpu.CompilerParams(vmem_limit_bytes=16 * 2**20),
        cost_estimate=pl.CostEstimate(flops=10**9, bytes_accessed=3 * 2**20, transcendentals=0),
    )(field, coupling, picks)
    came = travelled(out)
    gain, add = pl.pallas_call(
        first_local_kernel,
        out_shape=[jax.ShapeDtypeStruct((LOW * 8, LOW), jnp.float32)] * 2,
        scratch_shapes=[pltpu.VMEM((16, 32, 256), jnp.float32)],
        compiler_params=pltpu.CompilerParams(vmem_limit_bytes=16 * 2**20),
        cost_estimate=pl.CostEstimate(flops=3 * 10**9, bytes_accessed=4 * 2**20, transcendentals=0),
    )(
        field, coupling, advect[:, np.array(B_NODES)], trace, came, links,
        jnp.asarray(stacked3(near, 1)), bf(pick_b),
    )

    lanes = advect[:, np.array(B_NODES + I_NODES)].reshape(2, 2, 32, 2, LOW)
    lanes = lanes.transpose(0, 4, 1, 3, 2).reshape(2, LOW, LOW)
    own = lax.dynamic_slice_in_dim(lanes, 4 * lax.axis_index("span"), 4, axis=1)
    own_inner = jnp.concatenate([own[0, :, 64:], own[1, :, 64:]], axis=1)

    edge, inner = call(first_filter_kernel, [((32, 4, 8, LOW), jnp.float32)] * 2, 10**9)(arrived, high, low)
    edge_back = exchange(edge.reshape(LOW * 8, LOW))

    slope_inner = np.concatenate([slope_a[:, 64:], slope_b[:, 64:]], axis=1)
    inner = call(first_inner_kernel, [((32, 4, 8, LOW), jnp.float32)], 5 * 10**8)(
        arrived, inner, jnp.asarray(stacked3(slope_inner, 0)), own_inner
    )

    edge = edge_back * gain + add
    edge_there = exchange(edge).reshape(32, 4, 8, LOW)

    trace, out = call(
        second_traces_kernel, [((128, 1024), jnp.float32), ((64, 128), jnp.float32)], 5 * 10**8
    )(edge, picks)
    came = travelled(out)
    lift = call(second_local_kernel, [((16, 32, 256), jnp.float32)], 10**9)(trace, came, links)

    slope = np.concatenate([slope_a, slope_b], axis=1)
    value = call(second_filter_kernel, [((32, 4, 16, LOW), jnp.float32)], 2 * 10**9)(
        edge_there, inner, high, low, jnp.asarray(stacked3(slope, 0)), own,
        jnp.asarray(PEN * count[None, :], jnp.float32),
    )
    value = exchange(value.reshape(LOW * 16, LOW))
    return call(final_kernel, [((16, 64, 256), jnp.float32)], 2 * 10**8)(value, lift, bf(order.T))


def solution(mesh):
    placed = (
        P("span", None, "mesh"),
        P("span", None, "mesh"),
        P(None, None, "mesh"),
        P("mesh", None, None),
        P(None, "mesh"),
    )
    return jax.shard_map(shards, mesh=mesh, in_specs=placed, out_specs=P("span", None, "mesh"), check_vma=False)
```

time: 620 us -> 248 us (0.40); the launches traced: 611 us -> 247 us
  blocking collectives: 361 us -> 95.2 us
  local copies, waits for them, and re-layouts: 58.8 us -> 14 us
  matrix products: 33.6 us -> 0 us
  waiting for transfers between devices: 115 us -> 90.7 us
  Pallas kernels: 0 us -> 12.6 us
    all_to_all x6 -> x1, blocking collectives: 361 us -> 95.2 us  [exchange(): return lax.all_to_all(x, 'span', split_axis=0, concat_axis=0, tiled=True)]
    dot_general x8 -> x0, matrix products: 33.6 us -> none  [the longest x4 27.2 us: apply_table(): jnp.dot(table, flat, precision=lax.Precision.HIGHEST).reshape(block.shape)]
    all_to_all x2 -> x3, waiting for transfers between devices: 110 us -> 89.9 us  [exchange(): return lax.all_to_all(x, 'span', split_axis=0, concat_axis=0, tiled=True)]
    reshape x7 -> x2, local copies, waits for them, and re-layouts: 18.9 us -> 0.08 us  [shards(): lanes = advect[:, np.array(B_NODES + I_NODES)].reshape(2, 2, 32, 2, LOW)]
    pallas_call x0 -> x9, Pallas kernels: none -> 12.6 us  [the longest x7 10.4 us: run(): pl.pallas_call(kernel, out_shape=shapes if len(shapes) > 1 else shapes[0]...]
    unnamed x55 -> x50, local copies, waits for them, and re-layouts: 1.94 us -> 12.3 us
    all_to_all x15 -> x0, local copies, waits for them, and re-layouts: 9.05 us -> none  [the longest x8 3.37 us: shards(): lax.all_to_all(apply_table(table, lax.all_to_all(mixed, 'span', split_axi...]
    transpose x3 -> x0, local copies, waits for them, and re-layouts: 8.89 us -> none  [the longest x2 8.75 us: operate(): rows = own.transpose(3, 1, 2, 0).reshape(4 * elems, row_width)]
  transfers between devices with their start and end apart: 6 -> 7, of which waited for: 4 -> 4; matrix products, arithmetic and copies ran while one was open for 1% -> 1% of each run, Pallas kernels for 0% -> 2%
where the time goes in v1:
time: 248 us; the launch traced here: 247 us
  blocking collectives  95.2 us (38%)
  waiting for transfers between devices  90.7 us (37%)
  starting transfers between devices  31.1 us (13%)
  local copies, waits for them, and re-layouts  14 us (6%)
  Pallas kernels  12.6 us (5%)
  other arithmetic  3.21 us (1%)
    all_to_all x1, blocking collectives, exchange(): return lax.all_to_all(x, 'span', split_axis=0, concat_axis=0, tiled=True)  95.2 us
    all_to_all x3, waiting for transfers between devices, exchange(): return lax.all_to_all(x, 'span', split_axis=0, concat_axis=0, tiled=True)  89.9 us
    ppermute x4, starting transfers between devices, shifted(): lax.ppermute(block, 'mesh', [((i - distance) % devices, i) for i in range...  17.5 us
    all_to_all x3, starting transfers between devices, exchange(): return lax.all_to_all(x, 'span', split_axis=0, concat_axis=0, tiled=True)  13.5 us
    unnamed x50, local copies, waits for them, and re-layouts  12.3 us
    pallas_call x7, Pallas kernels, run(): pl.pallas_call(kernel, out_shape=shapes if len(shapes) > 1 else shapes[0]...  10.4 us
  transfers between devices with their start and end apart: 7, of which 4 were waited for; matrix products, arithmetic and copies ran while one was open for 1% of the time, Pallas kernels for 2%

profile of v1, /device:TPU:1, one launch (start us, length us, event | category | flops | bytes accessed | tf_op | source)
XLA Modules:
  0.0 247.2 jit_solution(5282401188222921987)
XLA Ops:
  0.0 1.3 copy-done.1
  1.3 1.2 copy-done.3
  3.2 0.8 shard_map.172
  4.1 95.2 %all_to_all.41 = f32[32,96,128]{2,1,0:T(8,128)S(1)} all-to-all(f32[32,96,128]{2,1,0:T(8,128)S(1)} %bitcast.35), channel_id=1, replica_groups=mesh['span'=32,'mesh'=16] {'span'}, dimensions={0} | all-to-all | bytes 3145728 | tf_op jit(solution)/shard_map/all_to_all | solution.py:316
  99.3 2.0 shard_map.173
  101.3 4.7 %all-to-all-start.1 = ((f32[32,32,128]{2,1,0:T(8,128)}), f32[32,32,128]{2,1,0:T(8,128)}, u32[]{:S(2)}, u32[]{:S(2)}) async-start(f32[32,32,128]{2,1,0:T(8,128)} %bitcast.2), calls=%async_computation.1 | async-start | bytes 1048576 | tf_op jit(solution)/shard_map/all_to_all | solution.py:316
  106.9 1.2 copy-done.4
  108.6 0.8 copy-done.19
  109.4 3.2 %collective-permute-start = (f32[32,128]{1,0:T(8,128)S(1)}, f32[32,128]{1,0:T(8,128)S(1)}, u32[]{:S(2)}, u32[]{:S(2)}) collective-permute-start(f32[32,128]{1,0:T(8,128)S(1)} %get-tuple-element.23), channel_id=1, source_target_pairs={{15,0},{0,1},{1,2},{2,3},{3,4},{4,5},{5,6},{6,7},{7,8},{8,9},{9,10... | collective-permute-start | bytes 49160 | tf_op jit(solution)/shard_map/ppermute | solution.py:321
  112.6 5.6 %collective-permute-start.1 = (f32[32,128]{1,0:T(8,128)S(1)}, f32[32,128]{1,0:T(8,128)S(1)}, u32[]{:S(2)}, u32[]{:S(2)}) collective-permute-start(f32[32,128]{1,0:T(8,128)S(1)} %get-tuple-element.24), channel_id=1, source_target_pairs={{1,0},{2,1},{3,2},{4,3},{5,4},{6,5},{7,6},{8,7},{9,8},{10,9},{11,1... | collective-permute-start | bytes 49160 | tf_op jit(solution)/shard_map/ppermute | solution.py:321
  119.0 1.2 copy-done.5
  120.3 1.0 copy-done.20
  121.3 1.8 shard_map.175
  123.2 0.8 copy-done.6
  124.0 0.8 copy-done.7
  124.8 14.8 %all-to-all-done.1 = f32[32,32,128]{2,1,0:T(8,128)} async-done(((f32[32,32,128]{2,1,0:T(8,128)}), f32[32,32,128]{2,1,0:T(8,128)}, u32[]{:S(2)}, u32[]{:S(2)}) %all-to-all-start.1) | async-done | bytes 524320 | tf_op jit(solution)/shard_map/all_to_all | solution.py:316
  139.6 2.2 fusion.value_ref
  141.8 4.5 %all-to-all-start.2 = ((f32[32,32,128]{2,1,0:T(8,128)}), f32[32,32,128]{2,1,0:T(8,128)S(1)}, u32[]{:S(2)}, u32[]{:S(2)}) async-start(f32[32,32,128]{2,1,0:T(8,128)} %bitcast.8), calls=%async_computation.2 | async-start | bytes 1048576 | tf_op jit(solution)/shard_map/all_to_all | solution.py:316
  146.3 0.8 gather_fusion.1
  148.2 31.6 %all-to-all-done.2 = f32[32,32,128]{2,1,0:T(8,128)S(1)} async-done(((f32[32,32,128]{2,1,0:T(8,128)}), f32[32,32,128]{2,1,0:T(8,128)S(1)}, u32[]{:S(2)}, u32[]{:S(2)}) %all-to-all-start.2) | async-done | bytes 524320 | tf_op jit(solution)/shard_map/all_to_all | solution.py:316
  179.9 1.0 copy-done.12
  180.9 1.0 copy-done.14
  181.9 0.9 copy-done.15
  182.9 2.6 %shard_map.177 = f32[32,4,16,128]{3,2,1,0:T(8,128)} custom-call(f32[32,4,8,128]{3,2,1,0:T(8,128)S(1)} %bitcast.37, f32[32,4,8,128]{3,2,1,0:T(8,128)S(1)} %shard_map.176.inner_ref, bf16[512,512]{1,0:T(8,128)(2,1)S(1)} %copy-done.12, bf16[512,512]{1,0:T(8,128)(2,1)S(1)} %copy-done.14, bf16[384,256]{1,0:T(8,128)(2,1)S(1)} %copy-done.15, ...), custom_call_target="tpu_custom_call" | custom-call | flops 2000000000 | bytes 3346944 | tf_op jit(solution)/shard_map/pallas_call | solution.py:115
  185.5 4.4 %all-to-all-start.3 = ((f32[32,64,128]{2,1,0:T(8,128)}), f32[32,64,128]{2,1,0:T(8,128)S(1)}, u32[]{:S(2)}, u32[]{:S(2)}) async-start(f32[32,64,128]{2,1,0:T(8,128)} %bitcast.15), calls=%async_computation.3 | async-start | bytes 2097152 | tf_op jit(solution)/shard_map/all_to_all | solution.py:316
  189.9 1.5 shard_map.178
  191.4 3.1 %collective-permute-start.2 = (f32[32,128]{1,0:T(8,128)S(1)}, f32[32,128]{1,0:T(8,128)S(1)}, u32[]{:S(2)}, u32[]{:S(2)}) collective-permute-start(f32[32,128]{1,0:T(8,128)S(1)} %get-tuple-element.21), channel_id=1, source_target_pairs={{15,0},{0,1},{1,2},{2,3},{3,4},{4,5},{5,6},{6,7},{7,8},{8,9},{9,10... | collective-permute-start | bytes 49160 | tf_op jit(solution)/shard_map/ppermute | solution.py:321
  194.5 5.6 %collective-permute-start.3 = (f32[32,128]{1,0:T(8,128)S(1)}, f32[32,128]{1,0:T(8,128)S(1)}, u32[]{:S(2)}, u32[]{:S(2)}) collective-permute-start(f32[32,128]{1,0:T(8,128)S(1)} %get-tuple-element.22), channel_id=1, source_target_pairs={{1,0},{2,1},{3,2},{4,3},{5,4},{6,5},{7,6},{8,7},{9,8},{10,9},{11,1... | collective-permute-start | bytes 49160 | tf_op jit(solution)/shard_map/ppermute | solution.py:321
  200.2 0.8 collective-permute-done.3
  201.0 1.2 shard_map.179.lift_ref
  202.3 43.4 %all-to-all-done.3 = f32[32,64,128]{2,1,0:T(8,128)S(1)} async-done(((f32[32,64,128]{2,1,0:T(8,128)}), f32[32,64,128]{2,1,0:T(8,128)S(1)}, u32[]{:S(2)}, u32[]{:S(2)}) %all-to-all-start.3) | async-done | bytes 1048608 | tf_op jit(solution)/shard_map/all_to_all | solution.py:316
  245.7 1.5 shard_map.180
  (60 shorter events, 4.0 us)
Async XLA Ops:
  0.0 118.3 %copy-start = (f32[2,64,256]{2,1,0:T(8,128)S(1)}, f32[2,64,256]{2,1,0:T(8,128)}, u32[]{:S(2)}) copy-start(f32[2,64,256]{2,1,0:T(8,128)} %param.20) | copy-start | bytes 393220
  0.0 1.3 copy-start.1
  1.3 1.2 copy-start.3
  2.5 0.8 copy-start.9
  4.0 95.2 %copy-start.11 = (bf16[512,512]{1,0:T(8,128)(2,1)S(1)}, bf16[512,512]{1,0:T(8,128)(2,1)}, u32[]{:S(2)}) copy-start(bf16[512,512]{1,0:T(8,128)(2,1)} %constant.146.clone.high_ref) | copy-start | bytes 1572868
  4.1 95.2 %copy-start.13 = (bf16[512,512]{1,0:T(8,128)(2,1)S(1)}, bf16[512,512]{1,0:T(8,128)(2,1)}, u32[]{:S(2)}) copy-start(bf16[512,512]{1,0:T(8,128)(2,1)} %constant.147.clone.low_ref) | copy-start | bytes 1572868
  99.3 7.6 %copy-start.2 = (f32[16,64,256]{2,1,0:T(8,128)S(1)}, f32[16,64,256]{2,1,0:T(8,128)}, u32[]{:S(2)}) copy-start(f32[16,64,256]{2,1,0:T(8,128)} %field_ref.5) | copy-start | bytes 3145732
  101.3 38.3 %all-to-all-start.1 = ((f32[32,32,128]{2,1,0:T(8,128)}), f32[32,32,128]{2,1,0:T(8,128)}, u32[]{:S(2)}, u32[]{:S(2)}) async-start(f32[32,32,128]{2,1,0:T(8,128)} %bitcast.2), calls=%async_computation.1 | async-start | bytes 1048576 | tf_op jit(solution)/shard_map/all_to_all | solution.py:316
  106.9 1.2 copy-start.4
  108.2 10.0 %copy-start.21 = (s32[4,256]{1,0:T(4,128)S(1)}, s32[4,256]{1,0:T(4,128)}, u32[]{:S(2)}) copy-start(s32[4,256]{1,0:T(4,128)} %param.22) | copy-start | bytes 12292
  108.2 10.1 %copy-start.23 = (s32[32]{0:T(128)S(1)}, s32[32]{0:T(128)}, u32[]{:S(2)}) copy-start(s32[32]{0:T(128)} %constant.167) | copy-start | bytes 388
  108.2 10.9 %copy-start.16 = (bf16[96,192]{1,0:T(8,128)(2,1)S(1)}, bf16[96,192]{1,0:T(8,128)(2,1)}, u32[]{:S(2)}) copy-start(bf16[96,192]{1,0:T(8,128)(2,1)} %constant.151.clone.near_ref) | copy-start | bytes 110596
  108.2 10.9 %copy-start.17 = (bf16[32,64]{1,0:T(8,128)(2,1)S(1)}, bf16[32,64]{1,0:T(8,128)(2,1)}, u32[]{:S(2)}) copy-start(bf16[32,64]{1,0:T(8,128)(2,1)} %constant.152.clone.pick_ref) | copy-start | bytes 12292
  108.6 0.8 copy-start.19
  109.4 9.6 %collective-permute-start = (f32[32,128]{1,0:T(8,128)S(1)}, f32[32,128]{1,0:T(8,128)S(1)}, u32[]{:S(2)}, u32[]{:S(2)}) collective-permute-start(f32[32,128]{1,0:T(8,128)S(1)} %get-tuple-element.23), channel_id=1, source_target_pairs={{15,0},{0,1},{1,2},{2,3},{3,4},{4,5},{5,6},{6,7},{7,8},{8,9},{9,10... | collective-permute-start | bytes 49160 | tf_op jit(solution)/shard_map/ppermute | solution.py:321
  112.6 6.4 %collective-permute-start.1 = (f32[32,128]{1,0:T(8,128)S(1)}, f32[32,128]{1,0:T(8,128)S(1)}, u32[]{:S(2)}, u32[]{:S(2)}) collective-permute-start(f32[32,128]{1,0:T(8,128)S(1)} %get-tuple-element.24), channel_id=1, source_target_pairs={{1,0},{2,1},{3,2},{4,3},{5,4},{6,5},{7,6},{8,7},{9,8},{10,9},{11,1... | collective-permute-start | bytes 49160 | tf_op jit(solution)/shard_map/ppermute | solution.py:321
  119.0 1.2 copy-start.5
  120.3 1.0 copy-start.20
  123.2 0.8 copy-start.6
  124.0 0.8 copy-start.7
  139.6 6.7 %copy-start.22 = (s32[64]{0:T(128)S(1)}, s32[64]{0:T(128)}, u32[]{:S(2)}) copy-start(s32[64]{0:T(128)} %constant.168) | copy-start | bytes 772
  141.8 5.7 %copy-start.8 = (bf16[384,128]{1,0:T(8,128)(2,1)S(1)}, bf16[384,128]{1,0:T(8,128)(2,1)}, u32[]{:S(2)}) copy-start(bf16[384,128]{1,0:T(8,128)(2,1)} %constant.154.clone.slope_ref) | copy-start | bytes 294916
  141.8 38.0 %all-to-all-start.2 = ((f32[32,32,128]{2,1,0:T(8,128)}), f32[32,32,128]{2,1,0:T(8,128)S(1)}, u32[]{:S(2)}, u32[]{:S(2)}) async-start(f32[32,32,128]{2,1,0:T(8,128)} %bitcast.8), calls=%async_computation.2 | async-start | bytes 1048576 | tf_op jit(solution)/shard_map/all_to_all | solution.py:316
  147.2 32.7 %copy-start.18 = (f32[1,128]{1,0:T(1,128)S(1)}, f32[1,128]{1,0:T(1,128)}, u32[]{:S(2)}) copy-start(f32[1,128]{1,0:T(1,128)} %constant.156.clone.count_ref) | copy-start | bytes 1540
  179.9 1.0 copy-start.12
  180.9 1.0 copy-start.14
  181.9 0.9 copy-start.15
  185.5 60.2 %all-to-all-start.3 = ((f32[32,64,128]{2,1,0:T(8,128)}), f32[32,64,128]{2,1,0:T(8,128)S(1)}, u32[]{:S(2)}, u32[]{:S(2)}) async-start(f32[32,64,128]{2,1,0:T(8,128)} %bitcast.15), calls=%async_computation.3 | async-start | bytes 2097152 | tf_op jit(solution)/shard_map/all_to_all | solution.py:316
  191.4 8.8 %collective-permute-start.2 = (f32[32,128]{1,0:T(8,128)S(1)}, f32[32,128]{1,0:T(8,128)S(1)}, u32[]{:S(2)}, u32[]{:S(2)}) collective-permute-start(f32[32,128]{1,0:T(8,128)S(1)} %get-tuple-element.21), channel_id=1, source_target_pairs={{15,0},{0,1},{1,2},{2,3},{3,4},{4,5},{5,6},{6,7},{7,8},{8,9},{9,10... | collective-permute-start | bytes 49160 | tf_op jit(solution)/shard_map/ppermute | solution.py:321
  194.5 6.5 %collective-permute-start.3 = (f32[32,128]{1,0:T(8,128)S(1)}, f32[32,128]{1,0:T(8,128)S(1)}, u32[]{:S(2)}, u32[]{:S(2)}) collective-permute-start(f32[32,128]{1,0:T(8,128)S(1)} %get-tuple-element.22), channel_id=1, source_target_pairs={{1,0},{2,1},{3,2},{4,3},{5,4},{6,5},{7,6},{8,7},{9,8},{10,9},{11,1... | collective-permute-start | bytes 49160 | tf_op jit(solution)/shard_map/ppermute | solution.py:321
  201.0 44.6 %copy-start.10 = (bf16[128,128]{1,0:T(8,128)(2,1)S(1)}, bf16[128,128]{1,0:T(8,128)(2,1)}, u32[]{:S(2)}) copy-start(bf16[128,128]{1,0:T(8,128)(2,1)} %constant.157.clone.back_ref) | copy-start | bytes 98308

commit v2 on v1

--- a/solution.py
+++ b/solution.py
@@ -409,6 +409,7 @@
     lift = call(second_local_kernel, [((16, 32, 256), jnp.float32)], 10**9)(trace, came, links)
 
     slope = np.concatenate([slope_a, slope_b], axis=1)
+    edge_there, lift = lax.optimization_barrier((edge_there, lift))
     value = call(second_filter_kernel, [((32, 4, 16, LOW), jnp.float32)], 2 * 10**9)(
         edge_there, inner, high, low, jnp.asarray(stacked3(slope, 0)), own,
         jnp.asarray(PEN * count[None, :], jnp.float32),

time: 248 us -> 243 us (0.980)
  blocking collectives: 95.2 us -> 154 us
  waiting for transfers between devices: 90.7 us -> 34.9 us
  starting transfers between devices: 31.1 us -> 26.5 us
  local copies, waits for them, and re-layouts: 14 us -> 11 us
    all_to_all x1 -> x2, blocking collectives: 95.2 us -> 154 us  [exchange(): return lax.all_to_all(x, 'span', split_axis=0, concat_axis=0, tiled=True)]
    all_to_all x3 -> x2, waiting for transfers between devices: 89.9 us -> 34.7 us  [exchange(): return lax.all_to_all(x, 'span', split_axis=0, concat_axis=0, tiled=True)]
    all_to_all x3 -> x2, starting transfers between devices: 13.5 us -> 9.04 us  [exchange(): return lax.all_to_all(x, 'span', split_axis=0, concat_axis=0, tiled=True)]
    unnamed x50, local copies, waits for them, and re-layouts: 12.3 us -> 9.26 us
  transfers between devices with their start and end apart: 7 -> 6, of which waited for: 4 -> 3; matrix products, arithmetic and copies ran while one was open for 1% -> 1% of each run, Pallas kernels for 2% -> 2%
where the time goes in v2:
time: 243 us; the launch traced here: 242 us
  blocking collectives  154 us (63%)
  waiting for transfers between devices  34.9 us (14%)
  starting transfers between devices  26.5 us (11%)
  Pallas kernels  11.7 us (5%)
  local copies, waits for them, and re-layouts  11 us (5%)
  other arithmetic  3.22 us (1%)
    all_to_all x2, blocking collectives, exchange(): return lax.all_to_all(x, 'span', split_axis=0, concat_axis=0, tiled=True)  154 us
    all_to_all x2, waiting for transfers between devices, exchange(): return lax.all_to_all(x, 'span', split_axis=0, concat_axis=0, tiled=True)  34.7 us
    ppermute x4, starting transfers between devices, shifted(): lax.ppermute(block, 'mesh', [((i - distance) % devices, i) for i in range...  17.5 us
    pallas_call x7, Pallas kernels, run(): pl.pallas_call(kernel, out_shape=shapes if len(shapes) > 1 else shapes[0]...  9.39 us
    unnamed x50, local copies, waits for them, and re-layouts  9.26 us
    all_to_all x2, starting transfers between devices, exchange(): return lax.all_to_all(x, 'span', split_axis=0, concat_axis=0, tiled=True)  9.04 us
  transfers between devices with their start and end apart: 6, of which 3 were waited for; matrix products, arithmetic and copies ran while one was open for 1% of the time, Pallas kernels for 2%

profile of v2, /device:TPU:1, one launch (start us, length us, event | category | flops | bytes accessed | tf_op | source)
XLA Modules:
  0.0 242.2 jit_solution(3384793177042489508)
XLA Ops:
  0.0 1.3 copy-done.1
  1.3 1.2 copy-done.3
  2.5 0.8 copy-done.9
  3.2 0.8 shard_map.172
  4.1 95.2 %all_to_all.41 = f32[32,96,128]{2,1,0:T(8,128)S(1)} all-to-all(f32[32,96,128]{2,1,0:T(8,128)S(1)} %bitcast.35), channel_id=1, replica_groups=mesh['span'=32,'mesh'=16] {'span'}, dimensions={0} | all-to-all | bytes 3145728 | tf_op jit(solution)/shard_map/all_to_all | solution.py:316
  99.3 2.0 shard_map.173
  101.3 4.7 %all-to-all-start.1 = ((f32[32,32,128]{2,1,0:T(8,128)}), f32[32,32,128]{2,1,0:T(8,128)}, u32[]{:S(2)}, u32[]{:S(2)}) async-start(f32[32,32,128]{2,1,0:T(8,128)} %bitcast.2), calls=%async_computation.1 | async-start | bytes 1048576 | tf_op jit(solution)/shard_map/all_to_all | solution.py:316
  106.0 0.7 fusion.6
  107.0 1.2 copy-done.4
  108.2 0.4 shard_map.174
  108.6 0.8 copy-done.19
  109.4 3.2 %collective-permute-start = (f32[32,128]{1,0:T(8,128)S(1)}, f32[32,128]{1,0:T(8,128)S(1)}, u32[]{:S(2)}, u32[]{:S(2)}) collective-permute-start(f32[32,128]{1,0:T(8,128)S(1)} %get-tuple-element.27), channel_id=1, source_target_pairs={{15,0},{0,1},{1,2},{2,3},{3,4},{4,5},{5,6},{6,7},{7,8},{8,9},{9,10... | collective-permute-start | bytes 49160 | tf_op jit(solution)/shard_map/ppermute | solution.py:321
  112.6 5.6 %collective-permute-start.1 = (f32[32,128]{1,0:T(8,128)S(1)}, f32[32,128]{1,0:T(8,128)S(1)}, u32[]{:S(2)}, u32[]{:S(2)}) collective-permute-start(f32[32,128]{1,0:T(8,128)S(1)} %get-tuple-element.28), channel_id=1, source_target_pairs={{1,0},{2,1},{3,2},{4,3},{5,4},{6,5},{7,6},{8,7},{9,8},{10,9},{11,1... | collective-permute-start | bytes 49160 | tf_op jit(solution)/shard_map/ppermute | solution.py:321
  118.3 0.7 gather_fusion
  119.1 1.2 copy-done.5
  120.3 1.0 copy-done.20
  121.3 1.9 shard_map.175
  123.2 0.8 copy-done.6
  124.0 0.8 copy-done.7
  124.8 14.8 %all-to-all-done.1 = f32[32,32,128]{2,1,0:T(8,128)} async-done(((f32[32,32,128]{2,1,0:T(8,128)}), f32[32,32,128]{2,1,0:T(8,128)}, u32[]{:S(2)}, u32[]{:S(2)}) %all-to-all-start.1) | async-done | bytes 524320 | tf_op jit(solution)/shard_map/all_to_all | solution.py:316
  139.6 2.2 fusion.value_ref
  141.8 4.3 %all-to-all-start.2 = ((f32[32,32,128]{2,1,0:T(8,128)}), f32[32,32,128]{2,1,0:T(8,128)S(1)}, u32[]{:S(2)}, u32[]{:S(2)}) async-start(f32[32,32,128]{2,1,0:T(8,128)} %bitcast.8), calls=%async_computation.2 | async-start | bytes 1048576 | tf_op jit(solution)/shard_map/all_to_all | solution.py:316
  146.2 0.8 gather_fusion.1
  147.4 1.5 shard_map.176
  149.0 3.1 %collective-permute-start.2 = (f32[32,128]{1,0:T(8,128)S(1)}, f32[32,128]{1,0:T(8,128)S(1)}, u32[]{:S(2)}, u32[]{:S(2)}) collective-permute-start(f32[32,128]{1,0:T(8,128)S(1)} %get-tuple-element.25), channel_id=1, source_target_pairs={{15,0},{0,1},{1,2},{2,3},{3,4},{4,5},{5,6},{6,7},{7,8},{8,9},{9,10... | collective-permute-start | bytes 49160 | tf_op jit(solution)/shard_map/ppermute | solution.py:321
  152.1 5.6 %collective-permute-start.3 = (f32[32,128]{1,0:T(8,128)S(1)}, f32[32,128]{1,0:T(8,128)S(1)}, u32[]{:S(2)}, u32[]{:S(2)}) collective-permute-start(f32[32,128]{1,0:T(8,128)S(1)} %get-tuple-element.26), channel_id=1, source_target_pairs={{1,0},{2,1},{3,2},{4,3},{5,4},{6,5},{7,6},{8,7},{9,8},{10,9},{11,1... | collective-permute-start | bytes 49160 | tf_op jit(solution)/shard_map/ppermute | solution.py:321
  157.8 0.6 shard_map.178.inner_ref
  158.7 1.2 shard_map.177.lift_ref
  159.9 19.9 %all-to-all-done.2 = f32[32,32,128]{2,1,0:T(8,128)S(1)} async-done(((f32[32,32,128]{2,1,0:T(8,128)}), f32[32,32,128]{2,1,0:T(8,128)S(1)}, u32[]{:S(2)}, u32[]{:S(2)}) %all-to-all-start.2) | async-done | bytes 524320 | tf_op jit(solution)/shard_map/all_to_all | solution.py:316
  179.8 1.6 shard_map.179
  181.4 59.3 %all_to_all.42 = f32[32,64,128]{2,1,0:T(8,128)S(1)} all-to-all(f32[32,64,128]{2,1,0:T(8,128)S(1)} %bitcast.37), channel_id=1, replica_groups=mesh['span'=32,'mesh'=16] {'span'}, dimensions={0} | all-to-all | bytes 2097152 | tf_op jit(solution)/shard_map/all_to_all | solution.py:316
  240.7 1.5 shard_map.180
  (59 shorter events, 1.0 us)
Async XLA Ops:
  0.0 118.3 %copy-start = (f32[2,64,256]{2,1,0:T(8,128)S(1)}, f32[2,64,256]{2,1,0:T(8,128)}, u32[]{:S(2)}) copy-start(f32[2,64,256]{2,1,0:T(8,128)} %param.20) | copy-start | bytes 393220
  0.0 1.3 copy-start.1
  1.3 1.2 copy-start.3
  2.5 0.8 copy-start.9
  4.0 95.2 %copy-start.11 = (bf16[512,512]{1,0:T(8,128)(2,1)S(1)}, bf16[512,512]{1,0:T(8,128)(2,1)}, u32[]{:S(2)}) copy-start(bf16[512,512]{1,0:T(8,128)(2,1)} %constant.146.clone.high_ref) | copy-start | bytes 1572868
  4.1 95.2 %copy-start.13 = (bf16[512,512]{1,0:T(8,128)(2,1)S(1)}, bf16[512,512]{1,0:T(8,128)(2,1)}, u32[]{:S(2)}) copy-start(bf16[512,512]{1,0:T(8,128)(2,1)} %constant.147.clone.low_ref) | copy-start | bytes 1572868
  99.3 7.7 %copy-start.2 = (f32[16,64,256]{2,1,0:T(8,128)S(1)}, f32[16,64,256]{2,1,0:T(8,128)}, u32[]{:S(2)}) copy-start(f32[16,64,256]{2,1,0:T(8,128)} %field_ref.5) | copy-start | bytes 3145732
  101.3 38.3 %all-to-all-start.1 = ((f32[32,32,128]{2,1,0:T(8,128)}), f32[32,32,128]{2,1,0:T(8,128)}, u32[]{:S(2)}, u32[]{:S(2)}) async-start(f32[32,32,128]{2,1,0:T(8,128)} %bitcast.2), calls=%async_computation.1 | async-start | bytes 1048576 | tf_op jit(solution)/shard_map/all_to_all | solution.py:316
  107.0 1.2 copy-start.4
  108.2 10.0 %copy-start.21 = (s32[4,256]{1,0:T(4,128)S(1)}, s32[4,256]{1,0:T(4,128)}, u32[]{:S(2)}) copy-start(s32[4,256]{1,0:T(4,128)} %param.22) | copy-start | bytes 12292
  108.2 10.1 %copy-start.23 = (s32[32]{0:T(128)S(1)}, s32[32]{0:T(128)}, u32[]{:S(2)}) copy-start(s32[32]{0:T(128)} %constant.167) | copy-start | bytes 388
  108.2 10.9 %copy-start.16 = (bf16[96,192]{1,0:T(8,128)(2,1)S(1)}, bf16[96,192]{1,0:T(8,128)(2,1)}, u32[]{:S(2)}) copy-start(bf16[96,192]{1,0:T(8,128)(2,1)} %constant.151.clone.near_ref) | copy-start | bytes 110596
  108.2 10.9 %copy-start.17 = (bf16[32,64]{1,0:T(8,128)(2,1)S(1)}, bf16[32,64]{1,0:T(8,128)(2,1)}, u32[]{:S(2)}) copy-start(bf16[32,64]{1,0:T(8,128)(2,1)} %constant.152.clone.pick_ref) | copy-start | bytes 12292
  108.6 0.8 copy-start.19
  109.4 9.6 %collective-permute-start = (f32[32,128]{1,0:T(8,128)S(1)}, f32[32,128]{1,0:T(8,128)S(1)}, u32[]{:S(2)}, u32[]{:S(2)}) collective-permute-start(f32[32,128]{1,0:T(8,128)S(1)} %get-tuple-element.27), channel_id=1, source_target_pairs={{15,0},{0,1},{1,2},{2,3},{3,4},{4,5},{5,6},{6,7},{7,8},{8,9},{9,10... | collective-permute-start | bytes 49160 | tf_op jit(solution)/shard_map/ppermute | solution.py:321
  112.6 6.4 %collective-permute-start.1 = (f32[32,128]{1,0:T(8,128)S(1)}, f32[32,128]{1,0:T(8,128)S(1)}, u32[]{:S(2)}, u32[]{:S(2)}) collective-permute-start(f32[32,128]{1,0:T(8,128)S(1)} %get-tuple-element.28), channel_id=1, source_target_pairs={{1,0},{2,1},{3,2},{4,3},{5,4},{6,5},{7,6},{8,7},{9,8},{10,9},{11,1... | collective-permute-start | bytes 49160 | tf_op jit(solution)/shard_map/ppermute | solution.py:321
  119.0 1.2 copy-start.5
  120.3 1.0 copy-start.20
  123.2 0.8 copy-start.6
  124.0 0.8 copy-start.7
  139.6 6.6 %copy-start.22 = (s32[64]{0:T(128)S(1)}, s32[64]{0:T(128)}, u32[]{:S(2)}) copy-start(s32[64]{0:T(128)} %constant.168) | copy-start | bytes 772
  141.8 37.9 %all-to-all-start.2 = ((f32[32,32,128]{2,1,0:T(8,128)}), f32[32,32,128]{2,1,0:T(8,128)S(1)}, u32[]{:S(2)}, u32[]{:S(2)}) async-start(f32[32,32,128]{2,1,0:T(8,128)} %bitcast.8), calls=%async_computation.2 | async-start | bytes 1048576 | tf_op jit(solution)/shard_map/all_to_all | solution.py:316
  147.0 10.8 %copy-start.8 = (bf16[384,128]{1,0:T(8,128)(2,1)S(1)}, bf16[384,128]{1,0:T(8,128)(2,1)}, u32[]{:S(2)}) copy-start(bf16[384,128]{1,0:T(8,128)(2,1)} %constant.154.clone.slope_ref) | copy-start | bytes 294916
  149.0 9.4 %collective-permute-start.2 = (f32[32,128]{1,0:T(8,128)S(1)}, f32[32,128]{1,0:T(8,128)S(1)}, u32[]{:S(2)}, u32[]{:S(2)}) collective-permute-start(f32[32,128]{1,0:T(8,128)S(1)} %get-tuple-element.25), channel_id=1, source_target_pairs={{15,0},{0,1},{1,2},{2,3},{3,4},{4,5},{5,6},{6,7},{7,8},{8,9},{9,10... | collective-permute-start | bytes 49160 | tf_op jit(solution)/shard_map/ppermute | solution.py:321
  152.1 6.5 %collective-permute-start.3 = (f32[32,128]{1,0:T(8,128)S(1)}, f32[32,128]{1,0:T(8,128)S(1)}, u32[]{:S(2)}, u32[]{:S(2)}) collective-permute-start(f32[32,128]{1,0:T(8,128)S(1)} %get-tuple-element.26), channel_id=1, source_target_pairs={{1,0},{2,1},{3,2},{4,3},{5,4},{6,5},{7,6},{8,7},{9,8},{10,9},{11,1... | collective-permute-start | bytes 49160 | tf_op jit(solution)/shard_map/ppermute | solution.py:321
  158.6 21.1 %copy-start.12 = (bf16[512,512]{1,0:T(8,128)(2,1)S(1)}, bf16[512,512]{1,0:T(8,128)(2,1)}, u32[]{:S(2)}) copy-start(bf16[512,512]{1,0:T(8,128)(2,1)} %constant.146.clone.high_ref) | copy-start | bytes 1572868
  158.6 21.1 %copy-start.14 = (bf16[512,512]{1,0:T(8,128)(2,1)S(1)}, bf16[512,512]{1,0:T(8,128)(2,1)}, u32[]{:S(2)}) copy-start(bf16[512,512]{1,0:T(8,128)(2,1)} %constant.147.clone.low_ref) | copy-start | bytes 1572868
  158.6 21.1 %copy-start.15 = (bf16[384,256]{1,0:T(8,128)(2,1)S(1)}, bf16[384,256]{1,0:T(8,128)(2,1)}, u32[]{:S(2)}) copy-start(bf16[384,256]{1,0:T(8,128)(2,1)} %constant.155.clone.slope_ref) | copy-start | bytes 589828
  158.6 21.1 %copy-start.18 = (f32[1,128]{1,0:T(1,128)S(1)}, f32[1,128]{1,0:T(1,128)}, u32[]{:S(2)}) copy-start(f32[1,128]{1,0:T(1,128)} %constant.156.clone.count_ref) | copy-start | bytes 1540
  181.4 59.3 %copy-start.10 = (bf16[128,128]{1,0:T(8,128)(2,1)S(1)}, bf16[128,128]{1,0:T(8,128)(2,1)}, u32[]{:S(2)}) copy-start(bf16[128,128]{1,0:T(8,128)(2,1)} %constant.157.clone.back_ref) | copy-start | bytes 98308

commit v3 on v2

--- a/solution.py
+++ b/solution.py
@@ -282,6 +282,10 @@
         v = (u + lanes_swapped(u)).reshape(32, 16, LOW)
         local = jnp.where(low_lanes, v[:, :8], v[:, 8:])
         out_ref[:, e] = (inner_ref[:, e] + local) * (1.0 + value_ref[:, e, pl.ds(16, 8), :])
+
+
+def combine_kernel(value_ref, gain_ref, add_ref, out_ref):
+    out_ref[...] = value_ref[...] * gain_ref[...] + add_ref[...]
 
 
 def second_filter_kernel(edge_ref, inner_ref, high_ref, low_ref, slope_ref, advect_ref, count_ref, out_ref):
@@ -363,7 +367,7 @@
     bf = lambda t: jnp.asarray(t, jnp.bfloat16)
     high, low = jnp.asarray(high), jnp.asarray(low)
 
-    packed = call(pack_kernel, [((LOW * 24, LOW), jnp.float32)], 2 * 10**8)(field, coupling, bf(order))
+    packed = call(pack_kernel, [((LOW * 24, LOW), jnp.float32)], 2 * 10**8, 60)(field, coupling, bf(order))
     arrived = exchange(packed).reshape(32, 4, 24, LOW)
 
     picks, links = link_tables(send_rows, neighbours)
@@ -399,7 +403,7 @@
         arrived, inner, jnp.asarray(stacked3(slope_inner, 0)), own_inner
     )
 
-    edge = edge_back * gain + add
+    edge = call(combine_kernel, [((LOW * 8, LOW), jnp.float32)], 10**6, 60)(edge_back, gain, add)
     edge_there = exchange(edge).reshape(32, 4, 8, LOW)
 
     trace, out = call(

time: 243 us -> 243 us (level)
  Pallas kernels: 11.7 us -> 15.6 us
    pallas_call x7 -> x8, Pallas kernels: 9.39 us -> 13.4 us  [run(): pl.pallas_call(kernel, out_shape=shapes if len(shapes) > 1 else shapes[0]...]
    unnamed x50 -> x46, local copies, waits for them, and re-layouts: 9.26 us -> 6.91 us
  transfers between devices with their start and end apart: 6 -> 6, of which waited for: 3 -> 3; matrix products, arithmetic and copies ran while one was open for 1% -> 2% of each run, Pallas kernels for 2% -> 2%
where the time goes in v3:
time: 243 us; the launch traced here: 242 us
  blocking collectives  155 us (64%)
  waiting for transfers between devices  32.9 us (14%)
  starting transfers between devices  26.7 us (11%)
  Pallas kernels  15.6 us (6%)
  local copies, waits for them, and re-layouts  10.9 us (4%)
    all_to_all x2, blocking collectives, exchange(): return lax.all_to_all(x, 'span', split_axis=0, concat_axis=0, tiled=True)  155 us
    all_to_all x2, waiting for transfers between devices, exchange(): return lax.all_to_all(x, 'span', split_axis=0, concat_axis=0, tiled=True)  32.6 us
    ppermute x4, starting transfers between devices, shifted(): lax.ppermute(block, 'mesh', [((i - distance) % devices, i) for i in range...  17.5 us
    pallas_call x8, Pallas kernels, run(): pl.pallas_call(kernel, out_shape=shapes if len(shapes) > 1 else shapes[0]...  13.4 us
    all_to_all x2, starting transfers between devices, exchange(): return lax.all_to_all(x, 'span', split_axis=0, concat_axis=0, tiled=True)  9.17 us
    unnamed x46, local copies, waits for them, and re-layouts  6.91 us
  transfers between devices with their start and end apart: 6, of which 3 were waited for; matrix products, arithmetic and copies ran while one was open for 2% of the time, Pallas kernels for 2%

profile of v3, /device:TPU:1, one launch (start us, length us, event | category | flops | bytes accessed | tf_op | source)
XLA Modules:
  0.0 242.1 jit_solution(2645613551709286270)
XLA Ops:
  0.0 3.6 %shard_map.172 = f32[3072,128]{1,0:T(8,128)} custom-call(f32[16,64,256]{2,1,0:T(8,128)} %field_ref.5, f32[16,64,256]{2,1,0:T(8,128)} %coupling_ref.5, bf16[128,128]{1,0:T(8,128)(2,1)} %constant.148.clone.order_ref), custom_call_target="tpu_custom_call" | custom-call | flops 200000000 | bytes 3702784 | tf_op jit(solution)/shard_map/pallas_call | solution.py:115
  3.6 95.4 %all_to_all.40 = f32[32,96,128]{2,1,0:T(8,128)S(1)} all-to-all(f32[32,96,128]{2,1,0:T(8,128)} %bitcast.37), channel_id=1, replica_groups=mesh['span'=32,'mesh'=16] {'span'}, dimensions={0} | all-to-all | bytes 3145728 | tf_op jit(solution)/shard_map/all_to_all | solution.py:320
  99.0 2.0 shard_map.173
  101.0 4.7 %all-to-all-start.1 = ((f32[32,32,128]{2,1,0:T(8,128)}), f32[32,32,128]{2,1,0:T(8,128)}, u32[]{:S(2)}, u32[]{:S(2)}) async-start(f32[32,32,128]{2,1,0:T(8,128)} %bitcast.2), calls=%async_computation.1 | async-start | bytes 1048576 | tf_op jit(solution)/shard_map/all_to_all | solution.py:320
  105.7 0.7 fusion.5
  106.7 1.2 copy-done.3
  108.3 0.8 copy-done.17
  109.1 3.2 %collective-permute-start = (f32[32,128]{1,0:T(8,128)S(1)}, f32[32,128]{1,0:T(8,128)S(1)}, u32[]{:S(2)}, u32[]{:S(2)}) collective-permute-start(f32[32,128]{1,0:T(8,128)S(1)} %get-tuple-element.27), channel_id=1, source_target_pairs={{15,0},{0,1},{1,2},{2,3},{3,4},{4,5},{5,6},{6,7},{7,8},{8,9},{9,10... | collective-permute-start | bytes 49160 | tf_op jit(solution)/shard_map/ppermute | solution.py:325
  112.3 5.6 %collective-permute-start.1 = (f32[32,128]{1,0:T(8,128)S(1)}, f32[32,128]{1,0:T(8,128)S(1)}, u32[]{:S(2)}, u32[]{:S(2)}) collective-permute-start(f32[32,128]{1,0:T(8,128)S(1)} %get-tuple-element.28), channel_id=1, source_target_pairs={{1,0},{2,1},{3,2},{4,3},{5,4},{6,5},{7,6},{8,7},{9,8},{10,9},{11,1... | collective-permute-start | bytes 49160 | tf_op jit(solution)/shard_map/ppermute | solution.py:325
  118.0 0.7 gather_fusion
  118.8 1.2 copy-done.4
  120.0 1.0 copy-done.18
  121.0 1.8 shard_map.175
  122.9 0.8 copy-done.5
  123.7 0.8 copy-done.6
  124.5 14.8 %all-to-all-done.1 = f32[32,32,128]{2,1,0:T(8,128)} async-done(((f32[32,32,128]{2,1,0:T(8,128)}), f32[32,32,128]{2,1,0:T(8,128)}, u32[]{:S(2)}, u32[]{:S(2)}) %all-to-all-start.1) | async-done | bytes 524320 | tf_op jit(solution)/shard_map/all_to_all | solution.py:320
  139.3 2.2 shard_map.176.value_ref
  141.5 4.5 %all-to-all-start.2 = ((f32[32,32,128]{2,1,0:T(8,128)}), f32[32,32,128]{2,1,0:T(8,128)S(1)}, u32[]{:S(2)}, u32[]{:S(2)}) async-start(f32[32,32,128]{2,1,0:T(8,128)} %bitcast.33), calls=%async_computation.2 | async-start | bytes 1048576 | tf_op jit(solution)/shard_map/all_to_all | solution.py:320
  146.1 0.8 gather_fusion.1
  146.8 0.7 reshape.280
  147.6 0.9 copy.24
  148.5 0.8 constant_dynamic-slice_fusion
  149.2 1.0 copy.26.advect_ref
  150.4 0.5 shard_map.177
  150.9 3.1 %collective-permute-start.2 = (f32[32,128]{1,0:T(8,128)S(1)}, f32[32,128]{1,0:T(8,128)S(1)}, u32[]{:S(2)}, u32[]{:S(2)}) collective-permute-start(f32[32,128]{1,0:T(8,128)S(1)} %get-tuple-element.25), channel_id=1, source_target_pairs={{15,0},{0,1},{1,2},{2,3},{3,4},{4,5},{5,6},{6,7},{7,8},{8,9},{9,10... | collective-permute-start | bytes 49160 | tf_op jit(solution)/shard_map/ppermute | solution.py:325
  154.0 5.6 %collective-permute-start.3 = (f32[32,128]{1,0:T(8,128)S(1)}, f32[32,128]{1,0:T(8,128)S(1)}, u32[]{:S(2)}, u32[]{:S(2)}) collective-permute-start(f32[32,128]{1,0:T(8,128)S(1)} %get-tuple-element.26), channel_id=1, source_target_pairs={{1,0},{2,1},{3,2},{4,3},{5,4},{6,5},{7,6},{8,7},{9,8},{10,9},{11,1... | collective-permute-start | bytes 49160 | tf_op jit(solution)/shard_map/ppermute | solution.py:325
  159.7 0.6 shard_map.179.inner_ref
  160.5 1.2 shard_map.178.lift_ref
  161.8 17.8 %all-to-all-done.2 = f32[32,32,128]{2,1,0:T(8,128)S(1)} async-done(((f32[32,32,128]{2,1,0:T(8,128)}), f32[32,32,128]{2,1,0:T(8,128)S(1)}, u32[]{:S(2)}, u32[]{:S(2)}) %all-to-all-start.2) | async-done | bytes 524320 | tf_op jit(solution)/shard_map/all_to_all | solution.py:320
  179.6 1.6 shard_map.180
  181.2 59.3 %all_to_all.41 = f32[32,64,128]{2,1,0:T(8,128)S(1)} all-to-all(f32[32,64,128]{2,1,0:T(8,128)S(1)} %bitcast.34), channel_id=1, replica_groups=mesh['span'=32,'mesh'=16] {'span'}, dimensions={0} | all-to-all | bytes 2097152 | tf_op jit(solution)/shard_map/all_to_all | solution.py:320
  240.5 1.5 shard_map.181
  (55 shorter events, 1.2 us)
Async XLA Ops:
  0.0 118.0 %copy-start = (f32[2,64,256]{2,1,0:T(8,128)S(1)}, f32[2,64,256]{2,1,0:T(8,128)}, u32[]{:S(2)}) copy-start(f32[2,64,256]{2,1,0:T(8,128)} %param.20) | copy-start | bytes 393220
  3.6 95.4 %copy-start.9 = (bf16[512,512]{1,0:T(8,128)(2,1)S(1)}, bf16[512,512]{1,0:T(8,128)(2,1)}, u32[]{:S(2)}) copy-start(bf16[512,512]{1,0:T(8,128)(2,1)} %constant.146.clone.high_ref) | copy-start | bytes 1572868
  3.6 95.4 %copy-start.11 = (bf16[512,512]{1,0:T(8,128)(2,1)S(1)}, bf16[512,512]{1,0:T(8,128)(2,1)}, u32[]{:S(2)}) copy-start(bf16[512,512]{1,0:T(8,128)(2,1)} %constant.147.clone.low_ref) | copy-start | bytes 1572868
  99.0 7.7 %copy-start.2 = (f32[16,64,256]{2,1,0:T(8,128)S(1)}, f32[16,64,256]{2,1,0:T(8,128)}, u32[]{:S(2)}) copy-start(f32[16,64,256]{2,1,0:T(8,128)} %field_ref.5) | copy-start | bytes 3145732
  101.0 38.3 %all-to-all-start.1 = ((f32[32,32,128]{2,1,0:T(8,128)}), f32[32,32,128]{2,1,0:T(8,128)}, u32[]{:S(2)}, u32[]{:S(2)}) async-start(f32[32,32,128]{2,1,0:T(8,128)} %bitcast.2), calls=%async_computation.1 | async-start | bytes 1048576 | tf_op jit(solution)/shard_map/all_to_all | solution.py:320
  106.7 1.2 copy-start.3
  107.9 10.0 %copy-start.19 = (s32[4,256]{1,0:T(4,128)S(1)}, s32[4,256]{1,0:T(4,128)}, u32[]{:S(2)}) copy-start(s32[4,256]{1,0:T(4,128)} %param.22) | copy-start | bytes 12292
  107.9 10.1 %copy-start.21 = (s32[32]{0:T(128)S(1)}, s32[32]{0:T(128)}, u32[]{:S(2)}) copy-start(s32[32]{0:T(128)} %constant.167) | copy-start | bytes 388
  107.9 10.9 %copy-start.14 = (bf16[96,192]{1,0:T(8,128)(2,1)S(1)}, bf16[96,192]{1,0:T(8,128)(2,1)}, u32[]{:S(2)}) copy-start(bf16[96,192]{1,0:T(8,128)(2,1)} %constant.151.clone.near_ref) | copy-start | bytes 110596
  107.9 10.9 %copy-start.15 = (bf16[32,64]{1,0:T(8,128)(2,1)S(1)}, bf16[32,64]{1,0:T(8,128)(2,1)}, u32[]{:S(2)}) copy-start(bf16[32,64]{1,0:T(8,128)(2,1)} %constant.152.clone.pick_ref) | copy-start | bytes 12292
  108.3 0.8 copy-start.17
  109.1 9.6 %collective-permute-start = (f32[32,128]{1,0:T(8,128)S(1)}, f32[32,128]{1,0:T(8,128)S(1)}, u32[]{:S(2)}, u32[]{:S(2)}) collective-permute-start(f32[32,128]{1,0:T(8,128)S(1)} %get-tuple-element.27), channel_id=1, source_target_pairs={{15,0},{0,1},{1,2},{2,3},{3,4},{4,5},{5,6},{6,7},{7,8},{8,9},{9,10... | collective-permute-start | bytes 49160 | tf_op jit(solution)/shard_map/ppermute | solution.py:325
  112.3 6.4 %collective-permute-start.1 = (f32[32,128]{1,0:T(8,128)S(1)}, f32[32,128]{1,0:T(8,128)S(1)}, u32[]{:S(2)}, u32[]{:S(2)}) collective-permute-start(f32[32,128]{1,0:T(8,128)S(1)} %get-tuple-element.28), channel_id=1, source_target_pairs={{1,0},{2,1},{3,2},{4,3},{5,4},{6,5},{7,6},{8,7},{9,8},{10,9},{11,1... | collective-permute-start | bytes 49160 | tf_op jit(solution)/shard_map/ppermute | solution.py:325
  118.8 1.2 copy-start.4
  120.0 1.0 copy-start.18
  122.9 0.8 copy-start.5
  123.7 0.8 copy-start.6
  139.3 6.7 %copy-start.20 = (s32[64]{0:T(128)S(1)}, s32[64]{0:T(128)}, u32[]{:S(2)}) copy-start(s32[64]{0:T(128)} %constant.168) | copy-start | bytes 772
  141.5 8.8 %copy-start.1 = (f32[1024,128]{1,0:T(8,128)S(1)}, f32[1024,128]{1,0:T(8,128)}, u32[]{:S(2)}) copy-start(f32[1024,128]{1,0:T(8,128)} %shard_map.176.value_ref) | copy-start | bytes 1572868
  141.5 38.0 %all-to-all-start.2 = ((f32[32,32,128]{2,1,0:T(8,128)}), f32[32,32,128]{2,1,0:T(8,128)S(1)}, u32[]{:S(2)}, u32[]{:S(2)}) async-start(f32[32,32,128]{2,1,0:T(8,128)} %bitcast.33), calls=%async_computation.2 | async-start | bytes 1048576 | tf_op jit(solution)/shard_map/all_to_all | solution.py:320
  146.8 12.8 %copy-start.7 = (bf16[384,128]{1,0:T(8,128)(2,1)S(1)}, bf16[384,128]{1,0:T(8,128)(2,1)}, u32[]{:S(2)}) copy-start(bf16[384,128]{1,0:T(8,128)(2,1)} %constant.154.clone.slope_ref) | copy-start | bytes 294916
  150.9 9.4 %collective-permute-start.2 = (f32[32,128]{1,0:T(8,128)S(1)}, f32[32,128]{1,0:T(8,128)S(1)}, u32[]{:S(2)}, u32[]{:S(2)}) collective-permute-start(f32[32,128]{1,0:T(8,128)S(1)} %get-tuple-element.25), channel_id=1, source_target_pairs={{15,0},{0,1},{1,2},{2,3},{3,4},{4,5},{5,6},{6,7},{7,8},{8,9},{9,10... | collective-permute-start | bytes 49160 | tf_op jit(solution)/shard_map/ppermute | solution.py:325
  154.0 6.5 %collective-permute-start.3 = (f32[32,128]{1,0:T(8,128)S(1)}, f32[32,128]{1,0:T(8,128)S(1)}, u32[]{:S(2)}, u32[]{:S(2)}) collective-permute-start(f32[32,128]{1,0:T(8,128)S(1)} %get-tuple-element.26), channel_id=1, source_target_pairs={{1,0},{2,1},{3,2},{4,3},{5,4},{6,5},{7,6},{8,7},{9,8},{10,9},{11,1... | collective-permute-start | bytes 49160 | tf_op jit(solution)/shard_map/ppermute | solution.py:325
  160.5 19.1 %copy-start.10 = (bf16[512,512]{1,0:T(8,128)(2,1)S(1)}, bf16[512,512]{1,0:T(8,128)(2,1)}, u32[]{:S(2)}) copy-start(bf16[512,512]{1,0:T(8,128)(2,1)} %constant.146.clone.high_ref) | copy-start | bytes 1572868
  160.5 19.1 %copy-start.12 = (bf16[512,512]{1,0:T(8,128)(2,1)S(1)}, bf16[512,512]{1,0:T(8,128)(2,1)}, u32[]{:S(2)}) copy-start(bf16[512,512]{1,0:T(8,128)(2,1)} %constant.147.clone.low_ref) | copy-start | bytes 1572868
  160.5 19.1 %copy-start.13 = (bf16[384,256]{1,0:T(8,128)(2,1)S(1)}, bf16[384,256]{1,0:T(8,128)(2,1)}, u32[]{:S(2)}) copy-start(bf16[384,256]{1,0:T(8,128)(2,1)} %constant.155.clone.slope_ref) | copy-start | bytes 589828
  160.5 19.1 %copy-start.16 = (f32[1,128]{1,0:T(1,128)S(1)}, f32[1,128]{1,0:T(1,128)}, u32[]{:S(2)}) copy-start(f32[1,128]{1,0:T(1,128)} %constant.156.clone.count_ref) | copy-start | bytes 1540
  181.2 59.3 %copy-start.8 = (bf16[128,128]{1,0:T(8,128)(2,1)S(1)}, bf16[128,128]{1,0:T(8,128)(2,1)}, u32[]{:S(2)}) copy-start(bf16[128,128]{1,0:T(8,128)(2,1)} %constant.157.clone.back_ref) | copy-start | bytes 98308

commit v4 on v2

--- a/solution.py
+++ b/solution.py
@@ -391,6 +391,7 @@
     own = lax.dynamic_slice_in_dim(lanes, 4 * lax.axis_index("span"), 4, axis=1)
     own_inner = jnp.concatenate([own[0, :, 64:], own[1, :, 64:]], axis=1)
 
+    arrived, gain, add, own, own_inner = lax.optimization_barrier((arrived, gain, add, own, own_inner))
     edge, inner = call(first_filter_kernel, [((32, 4, 8, LOW), jnp.float32)] * 2, 10**9)(arrived, high, low)
     edge_back = exchange(edge.reshape(LOW * 8, LOW))
 

time: 243 us -> 243 us (level)
  blocking collectives: 154 us -> 96.1 us
  waiting for transfers between devices: 34.9 us -> 74.4 us
  starting transfers between devices: 26.5 us -> 39 us
  local copies, waits for them, and re-layouts: 11 us -> 17.7 us
    all_to_all x2, blocking collectives: 154 us -> 96.1 us  [exchange(): return lax.all_to_all(x, 'span', split_axis=0, concat_axis=0, tiled=True)]
    all_to_all x2, waiting for transfers between devices: 34.7 us -> 74.2 us  [exchange(): return lax.all_to_all(x, 'span', split_axis=0, concat_axis=0, tiled=True)]
    all_to_all x2, starting transfers between devices: 9.04 us -> 21.3 us  [exchange(): return lax.all_to_all(x, 'span', split_axis=0, concat_axis=0, tiled=True)]
    reshape x2, local copies, waits for them, and re-layouts: 0.08 us -> 3.17 us  [shards(): lanes = advect[:, np.array(B_NODES + I_NODES)].reshape(2, 2, 32, 2, LOW)]
    unnamed x50 -> x49, local copies, waits for them, and re-layouts: 9.26 us -> 9.67 us
  transfers between devices with their start and end apart: 6 -> 6, of which waited for: 3 -> 3; matrix products, arithmetic and copies ran while one was open for 1% -> 4% of each run, Pallas kernels for 2% -> 2%
where the time goes in v4:
time: 243 us; the launch traced here: 241 us
  blocking collectives  96.1 us (40%)
  waiting for transfers between devices  74.4 us (31%)
  starting transfers between devices  39 us (16%)
  local copies, waits for them, and re-layouts  17.7 us (7%)
  Pallas kernels  12.1 us (5%)
    all_to_all x2, blocking collectives, exchange(): return lax.all_to_all(x, 'span', split_axis=0, concat_axis=0, tiled=True)  96.1 us
    all_to_all x2, waiting for transfers between devices, exchange(): return lax.all_to_all(x, 'span', split_axis=0, concat_axis=0, tiled=True)  74.2 us
    all_to_all x2, starting transfers between devices, exchange(): return lax.all_to_all(x, 'span', split_axis=0, concat_axis=0, tiled=True)  21.3 us
    ppermute x4, starting transfers between devices, shifted(): lax.ppermute(block, 'mesh', [((i - distance) % devices, i) for i in range...  17.7 us
    pallas_call x7, Pallas kernels, run(): pl.pallas_call(kernel, out_shape=shapes if len(shapes) > 1 else shapes[0]...  9.82 us
    unnamed x49, local copies, waits for them, and re-layouts  9.67 us
  transfers between devices with their start and end apart: 6, of which 3 were waited for; matrix products, arithmetic and copies ran while one was open for 4% of the time, Pallas kernels for 2%

profile of v4, /device:TPU:1, one launch (start us, length us, event | category | flops | bytes accessed | tf_op | source)
XLA Modules:
  0.0 241.4 jit_solution(2725285259307437119)
XLA Ops:
  0.0 1.3 copy-done.1
  1.3 1.2 copy-done.3
  2.5 0.8 copy-done.9
  3.2 2.0 shard_map.172
  5.2 16.9 %all-to-all-start = ((f32[32,96,128]{2,1,0:T(8,128)}), f32[32,96,128]{2,1,0:T(8,128)S(1)}, u32[]{:S(2)}, u32[]{:S(2)}) async-start(f32[32,96,128]{2,1,0:T(8,128)} %bitcast), calls=%async_computation | async-start | bytes 3145728 | tf_op jit(solution)/shard_map/all_to_all | solution.py:316
  23.1 1.2 copy-done.4
  24.8 3.3 %collective-permute-start = (f32[32,128]{1,0:T(8,128)S(1)}, f32[32,128]{1,0:T(8,128)S(1)}, u32[]{:S(2)}, u32[]{:S(2)}) collective-permute-start(f32[32,128]{1,0:T(8,128)S(1)} %get-tuple-element.37), channel_id=1, source_target_pairs={{15,0},{0,1},{1,2},{2,3},{3,4},{4,5},{5,6},{6,7},{7,8},{8,9},{9,10... | collective-permute-start | bytes 49160 | tf_op jit(solution)/shard_map/ppermute | solution.py:321
  28.1 5.6 %collective-permute-start.1 = (f32[32,128]{1,0:T(8,128)S(1)}, f32[32,128]{1,0:T(8,128)S(1)}, u32[]{:S(2)}, u32[]{:S(2)}) collective-permute-start(f32[32,128]{1,0:T(8,128)S(1)} %get-tuple-element.38), channel_id=1, source_target_pairs={{1,0},{2,1},{3,2},{4,3},{5,4},{6,5},{7,6},{8,7},{9,8},{10,9},{11,1... | collective-permute-start | bytes 49160 | tf_op jit(solution)/shard_map/ppermute | solution.py:321
  33.8 1.4 gather_fusion.1
  35.2 1.6 reshape.279
  36.8 1.6 copy.23
  38.3 1.7 constant_dynamic-slice_fusion
  40.0 1.0 copy.26.advect_ref
  42.0 1.2 copy-done.5
  43.2 1.0 copy-done.20
  44.2 1.8 shard_map.174
  46.1 0.8 copy-done.6
  46.9 53.1 %all-to-all-done = f32[32,96,128]{2,1,0:T(8,128)S(1)} async-done(((f32[32,96,128]{2,1,0:T(8,128)}), f32[32,96,128]{2,1,0:T(8,128)S(1)}, u32[]{:S(2)}, u32[]{:S(2)}) %all-to-all-start) | async-done | bytes 1572896 | tf_op jit(solution)/shard_map/all_to_all | solution.py:316
  100.0 1.0 copy-done.11
  101.0 1.0 copy-done.13
  102.0 1.2 shard_map.175
  103.3 36.8 %all_to_all.41 = f32[32,32,128]{2,1,0:T(8,128)S(1)} all-to-all(f32[32,32,128]{2,1,0:T(8,128)S(1)} %bitcast.38), channel_id=1, replica_groups=mesh['span'=32,'mesh'=16] {'span'}, dimensions={0} | all-to-all | bytes 1048576 | tf_op jit(solution)/shard_map/all_to_all | solution.py:316
  140.0 0.9 fusion.value_ref
  140.9 4.5 %all-to-all-start.2 = ((f32[32,32,128]{2,1,0:T(8,128)}), f32[32,32,128]{2,1,0:T(8,128)S(1)}, u32[]{:S(2)}, u32[]{:S(2)}) async-start(f32[32,32,128]{2,1,0:T(8,128)} %bitcast.13), calls=%async_computation.2 | async-start | bytes 1048576 | tf_op jit(solution)/shard_map/all_to_all | solution.py:316
  145.4 1.6 shard_map.176
  147.0 3.1 %collective-permute-start.2 = (f32[32,128]{1,0:T(8,128)S(1)}, f32[32,128]{1,0:T(8,128)S(1)}, u32[]{:S(2)}, u32[]{:S(2)}) collective-permute-start(f32[32,128]{1,0:T(8,128)S(1)} %get-tuple-element.35), channel_id=1, source_target_pairs={{15,0},{0,1},{1,2},{2,3},{3,4},{4,5},{5,6},{6,7},{7,8},{8,9},{9,10... | collective-permute-start | bytes 49160 | tf_op jit(solution)/shard_map/ppermute | solution.py:321
  150.1 5.6 %collective-permute-start.3 = (f32[32,128]{1,0:T(8,128)S(1)}, f32[32,128]{1,0:T(8,128)S(1)}, u32[]{:S(2)}, u32[]{:S(2)}) collective-permute-start(f32[32,128]{1,0:T(8,128)S(1)} %get-tuple-element.36), channel_id=1, source_target_pairs={{1,0},{2,1},{3,2},{4,3},{5,4},{6,5},{7,6},{8,7},{9,8},{10,9},{11,1... | collective-permute-start | bytes 49160 | tf_op jit(solution)/shard_map/ppermute | solution.py:321
  156.6 1.2 shard_map.177.lift_ref
  157.9 21.1 %all-to-all-done.2 = f32[32,32,128]{2,1,0:T(8,128)S(1)} async-done(((f32[32,32,128]{2,1,0:T(8,128)}), f32[32,32,128]{2,1,0:T(8,128)S(1)}, u32[]{:S(2)}, u32[]{:S(2)}) %all-to-all-start.2) | async-done | bytes 524320 | tf_op jit(solution)/shard_map/all_to_all | solution.py:316
  179.0 1.6 shard_map.179
  180.6 59.3 %all_to_all.42 = f32[32,64,128]{2,1,0:T(8,128)S(1)} all-to-all(f32[32,64,128]{2,1,0:T(8,128)S(1)} %bitcast.36), channel_id=1, replica_groups=mesh['span'=32,'mesh'=16] {'span'}, dimensions={0} | all-to-all | bytes 2097152 | tf_op jit(solution)/shard_map/all_to_all | solution.py:316
  239.9 1.5 shard_map.180
  (59 shorter events, 3.2 us)
Async XLA Ops:
  0.0 33.7 %copy-start = (f32[2,64,256]{2,1,0:T(8,128)S(1)}, f32[2,64,256]{2,1,0:T(8,128)}, u32[]{:S(2)}) copy-start(f32[2,64,256]{2,1,0:T(8,128)} %param.20) | copy-start | bytes 393220
  0.0 1.3 copy-start.1
  1.3 1.2 copy-start.3
  2.5 0.8 copy-start.9
  5.2 17.8 %copy-start.2 = (f32[16,64,256]{2,1,0:T(8,128)S(1)}, f32[16,64,256]{2,1,0:T(8,128)}, u32[]{:S(2)}) copy-start(f32[16,64,256]{2,1,0:T(8,128)} %field_ref.5) | copy-start | bytes 3145732
  5.2 94.7 %all-to-all-start = ((f32[32,96,128]{2,1,0:T(8,128)}), f32[32,96,128]{2,1,0:T(8,128)S(1)}, u32[]{:S(2)}, u32[]{:S(2)}) async-start(f32[32,96,128]{2,1,0:T(8,128)} %bitcast), calls=%async_computation | async-start | bytes 3145728 | tf_op jit(solution)/shard_map/all_to_all | solution.py:316
  23.1 1.2 copy-start.4
  24.3 9.4 %copy-start.21 = (s32[4,256]{1,0:T(4,128)S(1)}, s32[4,256]{1,0:T(4,128)}, u32[]{:S(2)}) copy-start(s32[4,256]{1,0:T(4,128)} %param.22) | copy-start | bytes 12292
  24.3 9.4 %copy-start.23 = (s32[64]{0:T(128)S(1)}, s32[64]{0:T(128)}, u32[]{:S(2)}) copy-start(s32[64]{0:T(128)} %constant.168) | copy-start | bytes 772
  24.7 16.4 %copy-start.19 = (f32[128,1024]{1,0:T(8,128)}, f32[128,1024]{1,0:T(8,128)S(1)}, u32[]{:S(2)}) copy-start(f32[128,1024]{1,0:T(8,128)S(1)} %get-tuple-element.20.trace_ref) | copy-start | bytes 1572868
  24.7 16.2 %copy-start.22 = (s32[32]{0:T(128)S(1)}, s32[32]{0:T(128)}, u32[]{:S(2)}) copy-start(s32[32]{0:T(128)} %constant.167) | copy-start | bytes 388
  24.8 17.2 %copy-start.16 = (bf16[96,192]{1,0:T(8,128)(2,1)S(1)}, bf16[96,192]{1,0:T(8,128)(2,1)}, u32[]{:S(2)}) copy-start(bf16[96,192]{1,0:T(8,128)(2,1)} %constant.151.clone.near_ref) | copy-start | bytes 110596
  24.8 17.2 %copy-start.17 = (bf16[32,64]{1,0:T(8,128)(2,1)S(1)}, bf16[32,64]{1,0:T(8,128)(2,1)}, u32[]{:S(2)}) copy-start(bf16[32,64]{1,0:T(8,128)(2,1)} %constant.152.clone.pick_ref) | copy-start | bytes 12292
  24.8 17.1 %collective-permute-start = (f32[32,128]{1,0:T(8,128)S(1)}, f32[32,128]{1,0:T(8,128)S(1)}, u32[]{:S(2)}, u32[]{:S(2)}) collective-permute-start(f32[32,128]{1,0:T(8,128)S(1)} %get-tuple-element.37), channel_id=1, source_target_pairs={{15,0},{0,1},{1,2},{2,3},{3,4},{4,5},{5,6},{6,7},{7,8},{8,9},{9,10... | collective-permute-start | bytes 49160 | tf_op jit(solution)/shard_map/ppermute | solution.py:321
  28.1 13.8 %collective-permute-start.1 = (f32[32,128]{1,0:T(8,128)S(1)}, f32[32,128]{1,0:T(8,128)S(1)}, u32[]{:S(2)}, u32[]{:S(2)}) collective-permute-start(f32[32,128]{1,0:T(8,128)S(1)} %get-tuple-element.38), channel_id=1, source_target_pairs={{1,0},{2,1},{3,2},{4,3},{5,4},{6,5},{7,6},{8,7},{9,8},{10,9},{11,1... | collective-permute-start | bytes 49160 | tf_op jit(solution)/shard_map/ppermute | solution.py:321
  41.9 1.2 copy-start.5
  43.2 1.0 copy-start.20
  46.1 0.8 copy-start.6
  99.9 1.0 copy-start.11
  101.0 1.0 copy-start.13
  102.0 38.0 %copy-start.7 = (f32[1024,128]{1,0:T(8,128)S(1)}, f32[1024,128]{1,0:T(8,128)}, u32[]{:S(2)}) copy-start(f32[1024,128]{1,0:T(8,128)} %copy-done.6) | copy-start | bytes 1572868
  140.9 14.8 %copy-start.8 = (bf16[384,128]{1,0:T(8,128)(2,1)S(1)}, bf16[384,128]{1,0:T(8,128)(2,1)}, u32[]{:S(2)}) copy-start(bf16[384,128]{1,0:T(8,128)(2,1)} %constant.154.clone.slope_ref) | copy-start | bytes 294916
  140.9 38.0 %all-to-all-start.2 = ((f32[32,32,128]{2,1,0:T(8,128)}), f32[32,32,128]{2,1,0:T(8,128)S(1)}, u32[]{:S(2)}, u32[]{:S(2)}) async-start(f32[32,32,128]{2,1,0:T(8,128)} %bitcast.13), calls=%async_computation.2 | async-start | bytes 1048576 | tf_op jit(solution)/shard_map/all_to_all | solution.py:316
  147.0 9.4 %collective-permute-start.2 = (f32[32,128]{1,0:T(8,128)S(1)}, f32[32,128]{1,0:T(8,128)S(1)}, u32[]{:S(2)}, u32[]{:S(2)}) collective-permute-start(f32[32,128]{1,0:T(8,128)S(1)} %get-tuple-element.35), channel_id=1, source_target_pairs={{15,0},{0,1},{1,2},{2,3},{3,4},{4,5},{5,6},{6,7},{7,8},{8,9},{9,10... | collective-permute-start | bytes 49160 | tf_op jit(solution)/shard_map/ppermute | solution.py:321
  150.1 6.5 %collective-permute-start.3 = (f32[32,128]{1,0:T(8,128)S(1)}, f32[32,128]{1,0:T(8,128)S(1)}, u32[]{:S(2)}, u32[]{:S(2)}) collective-permute-start(f32[32,128]{1,0:T(8,128)S(1)} %get-tuple-element.36), channel_id=1, source_target_pairs={{1,0},{2,1},{3,2},{4,3},{5,4},{6,5},{7,6},{8,7},{9,8},{10,9},{11,1... | collective-permute-start | bytes 49160 | tf_op jit(solution)/shard_map/ppermute | solution.py:321
  156.6 22.3 %copy-start.12 = (bf16[512,512]{1,0:T(8,128)(2,1)S(1)}, bf16[512,512]{1,0:T(8,128)(2,1)}, u32[]{:S(2)}) copy-start(bf16[512,512]{1,0:T(8,128)(2,1)} %constant.147.clone.low_ref) | copy-start | bytes 1572868
  156.6 22.3 %copy-start.14 = (bf16[512,512]{1,0:T(8,128)(2,1)S(1)}, bf16[512,512]{1,0:T(8,128)(2,1)}, u32[]{:S(2)}) copy-start(bf16[512,512]{1,0:T(8,128)(2,1)} %constant.146.clone.high_ref) | copy-start | bytes 1572868
  156.6 22.3 %copy-start.15 = (bf16[384,256]{1,0:T(8,128)(2,1)S(1)}, bf16[384,256]{1,0:T(8,128)(2,1)}, u32[]{:S(2)}) copy-start(bf16[384,256]{1,0:T(8,128)(2,1)} %constant.155.clone.slope_ref) | copy-start | bytes 589828
  156.6 22.3 %copy-start.18 = (f32[1,128]{1,0:T(1,128)S(1)}, f32[1,128]{1,0:T(1,128)}, u32[]{:S(2)}) copy-start(f32[1,128]{1,0:T(1,128)} %constant.156.clone.count_ref) | copy-start | bytes 1540
  180.6 59.3 %copy-start.10 = (bf16[128,128]{1,0:T(8,128)(2,1)S(1)}, bf16[128,128]{1,0:T(8,128)(2,1)}, u32[]{:S(2)}) copy-start(bf16[128,128]{1,0:T(8,128)(2,1)} %constant.157.clone.back_ref) | copy-start | bytes 98308

commit v5 on v4

--- a/solution.py
+++ b/solution.py
@@ -363,7 +363,7 @@
     bf = lambda t: jnp.asarray(t, jnp.bfloat16)
     high, low = jnp.asarray(high), jnp.asarray(low)
 
-    packed = call(pack_kernel, [((LOW * 24, LOW), jnp.float32)], 2 * 10**8)(field, coupling, bf(order))
+    packed = call(pack_kernel, [((LOW * 24, LOW), jnp.float32)], 2 * 10**8, 60)(field, coupling, bf(order))
     arrived = exchange(packed).reshape(32, 4, 24, LOW)
 
     picks, links = link_tables(send_rows, neighbours)

time: 243 us -> 241 us (level)
  local copies, waits for them, and re-layouts: 17.7 us -> 14.5 us
    unnamed x49 -> x43, local copies, waits for them, and re-layouts: 9.67 us -> 6.43 us
where the time goes in v5:
time: 241 us; the launch traced here: 240 us
  blocking collectives  96.1 us (40%)
  waiting for transfers between devices  74.4 us (31%)
  starting transfers between devices  39 us (16%)
  local copies, waits for them, and re-layouts  14.5 us (6%)
  Pallas kernels  13.6 us (6%)
    all_to_all x2, blocking collectives, exchange(): return lax.all_to_all(x, 'span', split_axis=0, concat_axis=0, tiled=True)  96.1 us
    all_to_all x2, waiting for transfers between devices, exchange(): return lax.all_to_all(x, 'span', split_axis=0, concat_axis=0, tiled=True)  74.2 us
    all_to_all x2, starting transfers between devices, exchange(): return lax.all_to_all(x, 'span', split_axis=0, concat_axis=0, tiled=True)  21.3 us
    ppermute x4, starting transfers between devices, shifted(): lax.ppermute(block, 'mesh', [((i - distance) % devices, i) for i in range...  17.7 us
    pallas_call x7, Pallas kernels, run(): pl.pallas_call(kernel, out_shape=shapes if len(shapes) > 1 else shapes[0]...  11.4 us
    unnamed x43, local copies, waits for them, and re-layouts  6.43 us
  transfers between devices with their start and end apart: 6, of which 3 were waited for; matrix products, arithmetic and copies ran while one was open for 4% of the time, Pallas kernels for 2%

profile of v5, /device:TPU:1, one launch (start us, length us, event | category | flops | bytes accessed | tf_op | source)
XLA Modules:
  0.0 239.7 jit_solution(4020819951569696931)
XLA Ops:
  0.0 3.5 %shard_map.172 = f32[3072,128]{1,0:T(8,128)} custom-call(f32[16,64,256]{2,1,0:T(8,128)} %field_ref.5, f32[16,64,256]{2,1,0:T(8,128)} %coupling_ref.5, bf16[128,128]{1,0:T(8,128)(2,1)} %constant.148.clone.order_ref), custom_call_target="tpu_custom_call" | custom-call | flops 200000000 | bytes 3702784 | tf_op jit(solution)/shard_map/pallas_call | solution.py:115
  3.6 16.9 %all-to-all-start = ((f32[32,96,128]{2,1,0:T(8,128)}), f32[32,96,128]{2,1,0:T(8,128)S(1)}, u32[]{:S(2)}, u32[]{:S(2)}) async-start(f32[32,96,128]{2,1,0:T(8,128)} %bitcast.40), calls=%async_computation | async-start | bytes 3145728 | tf_op jit(solution)/shard_map/all_to_all | solution.py:316
  20.5 0.7 fusion.6
  21.4 1.2 copy-done.2
  23.1 3.3 %collective-permute-start = (f32[32,128]{1,0:T(8,128)S(1)}, f32[32,128]{1,0:T(8,128)S(1)}, u32[]{:S(2)}, u32[]{:S(2)}) collective-permute-start(f32[32,128]{1,0:T(8,128)S(1)} %get-tuple-element.37), channel_id=1, source_target_pairs={{15,0},{0,1},{1,2},{2,3},{3,4},{4,5},{5,6},{6,7},{7,8},{8,9},{9,10... | collective-permute-start | bytes 49160 | tf_op jit(solution)/shard_map/ppermute | solution.py:321
  26.4 5.6 %collective-permute-start.1 = (f32[32,128]{1,0:T(8,128)S(1)}, f32[32,128]{1,0:T(8,128)S(1)}, u32[]{:S(2)}, u32[]{:S(2)}) collective-permute-start(f32[32,128]{1,0:T(8,128)S(1)} %get-tuple-element.38), channel_id=1, source_target_pairs={{1,0},{2,1},{3,2},{4,3},{5,4},{6,5},{7,6},{8,7},{9,8},{10,9},{11,1... | collective-permute-start | bytes 49160 | tf_op jit(solution)/shard_map/ppermute | solution.py:321
  32.1 1.4 gather_fusion.1
  33.5 1.6 reshape.279
  35.1 1.6 copy.23
  36.7 1.7 constant_dynamic-slice_fusion
  38.3 1.0 copy.26.advect_ref
  39.6 0.7 gather_fusion
  40.3 1.2 copy-done.3
  41.5 1.0 copy-done.17
  42.5 1.8 shard_map.174
  44.4 0.8 copy-done.4
  45.2 53.1 %all-to-all-done = f32[32,96,128]{2,1,0:T(8,128)S(1)} async-done(((f32[32,96,128]{2,1,0:T(8,128)}), f32[32,96,128]{2,1,0:T(8,128)S(1)}, u32[]{:S(2)}, u32[]{:S(2)}) %all-to-all-start) | async-done | bytes 1572896 | tf_op jit(solution)/shard_map/all_to_all | solution.py:316
  98.3 1.0 copy-done.8
  99.3 1.0 copy-done.10
  100.3 1.2 shard_map.175
  101.6 36.8 %all_to_all.41 = f32[32,32,128]{2,1,0:T(8,128)S(1)} all-to-all(f32[32,32,128]{2,1,0:T(8,128)S(1)} %bitcast.38), channel_id=1, replica_groups=mesh['span'=32,'mesh'=16] {'span'}, dimensions={0} | all-to-all | bytes 1048576 | tf_op jit(solution)/shard_map/all_to_all | solution.py:316
  138.4 0.9 fusion.value_ref
  139.2 4.5 %all-to-all-start.2 = ((f32[32,32,128]{2,1,0:T(8,128)}), f32[32,32,128]{2,1,0:T(8,128)S(1)}, u32[]{:S(2)}, u32[]{:S(2)}) async-start(f32[32,32,128]{2,1,0:T(8,128)} %bitcast.13), calls=%async_computation.2 | async-start | bytes 1048576 | tf_op jit(solution)/shard_map/all_to_all | solution.py:316
  143.7 1.6 shard_map.176
  145.3 3.1 %collective-permute-start.2 = (f32[32,128]{1,0:T(8,128)S(1)}, f32[32,128]{1,0:T(8,128)S(1)}, u32[]{:S(2)}, u32[]{:S(2)}) collective-permute-start(f32[32,128]{1,0:T(8,128)S(1)} %get-tuple-element.35), channel_id=1, source_target_pairs={{15,0},{0,1},{1,2},{2,3},{3,4},{4,5},{5,6},{6,7},{7,8},{8,9},{9,10... | collective-permute-start | bytes 49160 | tf_op jit(solution)/shard_map/ppermute | solution.py:321
  148.4 5.6 %collective-permute-start.3 = (f32[32,128]{1,0:T(8,128)S(1)}, f32[32,128]{1,0:T(8,128)S(1)}, u32[]{:S(2)}, u32[]{:S(2)}) collective-permute-start(f32[32,128]{1,0:T(8,128)S(1)} %get-tuple-element.36), channel_id=1, source_target_pairs={{1,0},{2,1},{3,2},{4,3},{5,4},{6,5},{7,6},{8,7},{9,8},{10,9},{11,1... | collective-permute-start | bytes 49160 | tf_op jit(solution)/shard_map/ppermute | solution.py:321
  154.1 0.6 shard_map.178.inner_ref
  154.9 1.2 shard_map.177.lift_ref
  156.2 21.1 %all-to-all-done.2 = f32[32,32,128]{2,1,0:T(8,128)S(1)} async-done(((f32[32,32,128]{2,1,0:T(8,128)}), f32[32,32,128]{2,1,0:T(8,128)S(1)}, u32[]{:S(2)}, u32[]{:S(2)}) %all-to-all-start.2) | async-done | bytes 524320 | tf_op jit(solution)/shard_map/all_to_all | solution.py:316
  177.3 1.6 shard_map.179
  178.9 59.3 %all_to_all.42 = f32[32,64,128]{2,1,0:T(8,128)S(1)} all-to-all(f32[32,64,128]{2,1,0:T(8,128)S(1)} %bitcast.36), channel_id=1, replica_groups=mesh['span'=32,'mesh'=16] {'span'}, dimensions={0} | all-to-all | bytes 2097152 | tf_op jit(solution)/shard_map/all_to_all | solution.py:316
  238.2 1.5 shard_map.180
  (53 shorter events, 1.1 us)
Async XLA Ops:
  0.0 32.1 %copy-start = (f32[2,64,256]{2,1,0:T(8,128)S(1)}, f32[2,64,256]{2,1,0:T(8,128)}, u32[]{:S(2)}) copy-start(f32[2,64,256]{2,1,0:T(8,128)} %param.20) | copy-start | bytes 393220
  3.6 17.8 %copy-start.1 = (f32[16,64,256]{2,1,0:T(8,128)S(1)}, f32[16,64,256]{2,1,0:T(8,128)}, u32[]{:S(2)}) copy-start(f32[16,64,256]{2,1,0:T(8,128)} %field_ref.5) | copy-start | bytes 3145732
  3.6 94.7 %all-to-all-start = ((f32[32,96,128]{2,1,0:T(8,128)}), f32[32,96,128]{2,1,0:T(8,128)S(1)}, u32[]{:S(2)}, u32[]{:S(2)}) async-start(f32[32,96,128]{2,1,0:T(8,128)} %bitcast.40), calls=%async_computation | async-start | bytes 3145728 | tf_op jit(solution)/shard_map/all_to_all | solution.py:316
  21.4 1.2 copy-start.2
  22.6 9.4 %copy-start.18 = (s32[4,256]{1,0:T(4,128)S(1)}, s32[4,256]{1,0:T(4,128)}, u32[]{:S(2)}) copy-start(s32[4,256]{1,0:T(4,128)} %param.22) | copy-start | bytes 12292
  22.6 9.4 %copy-start.20 = (s32[64]{0:T(128)S(1)}, s32[64]{0:T(128)}, u32[]{:S(2)}) copy-start(s32[64]{0:T(128)} %constant.168) | copy-start | bytes 772
  23.0 16.4 %copy-start.16 = (f32[128,1024]{1,0:T(8,128)}, f32[128,1024]{1,0:T(8,128)S(1)}, u32[]{:S(2)}) copy-start(f32[128,1024]{1,0:T(8,128)S(1)} %get-tuple-element.20.trace_ref) | copy-start | bytes 1572868
  23.0 16.2 %copy-start.19 = (s32[32]{0:T(128)S(1)}, s32[32]{0:T(128)}, u32[]{:S(2)}) copy-start(s32[32]{0:T(128)} %constant.167) | copy-start | bytes 388
  23.1 17.2 %copy-start.13 = (bf16[96,192]{1,0:T(8,128)(2,1)S(1)}, bf16[96,192]{1,0:T(8,128)(2,1)}, u32[]{:S(2)}) copy-start(bf16[96,192]{1,0:T(8,128)(2,1)} %constant.151.clone.near_ref) | copy-start | bytes 110596
  23.1 17.2 %copy-start.14 = (bf16[32,64]{1,0:T(8,128)(2,1)S(1)}, bf16[32,64]{1,0:T(8,128)(2,1)}, u32[]{:S(2)}) copy-start(bf16[32,64]{1,0:T(8,128)(2,1)} %constant.152.clone.pick_ref) | copy-start | bytes 12292
  23.1 17.1 %collective-permute-start = (f32[32,128]{1,0:T(8,128)S(1)}, f32[32,128]{1,0:T(8,128)S(1)}, u32[]{:S(2)}, u32[]{:S(2)}) collective-permute-start(f32[32,128]{1,0:T(8,128)S(1)} %get-tuple-element.37), channel_id=1, source_target_pairs={{15,0},{0,1},{1,2},{2,3},{3,4},{4,5},{5,6},{6,7},{7,8},{8,9},{9,10... | collective-permute-start | bytes 49160 | tf_op jit(solution)/shard_map/ppermute | solution.py:321
  26.4 13.8 %collective-permute-start.1 = (f32[32,128]{1,0:T(8,128)S(1)}, f32[32,128]{1,0:T(8,128)S(1)}, u32[]{:S(2)}, u32[]{:S(2)}) collective-permute-start(f32[32,128]{1,0:T(8,128)S(1)} %get-tuple-element.38), channel_id=1, source_target_pairs={{1,0},{2,1},{3,2},{4,3},{5,4},{6,5},{7,6},{8,7},{9,8},{10,9},{11,1... | collective-permute-start | bytes 49160 | tf_op jit(solution)/shard_map/ppermute | solution.py:321
  40.3 1.2 copy-start.3
  41.5 1.0 copy-start.17
  44.4 0.8 copy-start.4
  98.3 1.0 copy-start.8
  99.3 1.0 copy-start.10
  100.3 38.0 %copy-start.5 = (f32[1024,128]{1,0:T(8,128)S(1)}, f32[1024,128]{1,0:T(8,128)}, u32[]{:S(2)}) copy-start(f32[1024,128]{1,0:T(8,128)} %copy-done.4) | copy-start | bytes 1572868
  139.2 14.8 %copy-start.6 = (bf16[384,128]{1,0:T(8,128)(2,1)S(1)}, bf16[384,128]{1,0:T(8,128)(2,1)}, u32[]{:S(2)}) copy-start(bf16[384,128]{1,0:T(8,128)(2,1)} %constant.154.clone.slope_ref) | copy-start | bytes 294916
  139.2 38.0 %all-to-all-start.2 = ((f32[32,32,128]{2,1,0:T(8,128)}), f32[32,32,128]{2,1,0:T(8,128)S(1)}, u32[]{:S(2)}, u32[]{:S(2)}) async-start(f32[32,32,128]{2,1,0:T(8,128)} %bitcast.13), calls=%async_computation.2 | async-start | bytes 1048576 | tf_op jit(solution)/shard_map/all_to_all | solution.py:316
  145.3 9.4 %collective-permute-start.2 = (f32[32,128]{1,0:T(8,128)S(1)}, f32[32,128]{1,0:T(8,128)S(1)}, u32[]{:S(2)}, u32[]{:S(2)}) collective-permute-start(f32[32,128]{1,0:T(8,128)S(1)} %get-tuple-element.35), channel_id=1, source_target_pairs={{15,0},{0,1},{1,2},{2,3},{3,4},{4,5},{5,6},{6,7},{7,8},{8,9},{9,10... | collective-permute-start | bytes 49160 | tf_op jit(solution)/shard_map/ppermute | solution.py:321
  148.4 6.5 %collective-permute-start.3 = (f32[32,128]{1,0:T(8,128)S(1)}, f32[32,128]{1,0:T(8,128)S(1)}, u32[]{:S(2)}, u32[]{:S(2)}) collective-permute-start(f32[32,128]{1,0:T(8,128)S(1)} %get-tuple-element.36), channel_id=1, source_target_pairs={{1,0},{2,1},{3,2},{4,3},{5,4},{6,5},{7,6},{8,7},{9,8},{10,9},{11,1... | collective-permute-start | bytes 49160 | tf_op jit(solution)/shard_map/ppermute | solution.py:321
  154.9 22.3 %copy-start.9 = (bf16[512,512]{1,0:T(8,128)(2,1)S(1)}, bf16[512,512]{1,0:T(8,128)(2,1)}, u32[]{:S(2)}) copy-start(bf16[512,512]{1,0:T(8,128)(2,1)} %constant.147.clone.low_ref) | copy-start | bytes 1572868
  154.9 22.3 %copy-start.11 = (bf16[512,512]{1,0:T(8,128)(2,1)S(1)}, bf16[512,512]{1,0:T(8,128)(2,1)}, u32[]{:S(2)}) copy-start(bf16[512,512]{1,0:T(8,128)(2,1)} %constant.146.clone.high_ref) | copy-start | bytes 1572868
  154.9 22.3 %copy-start.12 = (bf16[384,256]{1,0:T(8,128)(2,1)S(1)}, bf16[384,256]{1,0:T(8,128)(2,1)}, u32[]{:S(2)}) copy-start(bf16[384,256]{1,0:T(8,128)(2,1)} %constant.155.clone.slope_ref) | copy-start | bytes 589828
  154.9 22.3 %copy-start.15 = (f32[1,128]{1,0:T(1,128)S(1)}, f32[1,128]{1,0:T(1,128)}, u32[]{:S(2)}) copy-start(f32[1,128]{1,0:T(1,128)} %constant.156.clone.count_ref) | copy-start | bytes 1540
  178.9 59.3 %copy-start.7 = (bf16[128,128]{1,0:T(8,128)(2,1)S(1)}, bf16[128,128]{1,0:T(8,128)(2,1)}, u32[]{:S(2)}) copy-start(bf16[128,128]{1,0:T(8,128)(2,1)} %constant.157.clone.back_ref) | copy-start | bytes 98308
